TPU v7x, 32 devices: a whole 2x2x4 slice. The times are simulated.
32 devices in a mesh: face: 4 (over y, x), sub: 8 (over z, core).
Axes of the slice: x: 2, y: 2, z: 4, core: 2. Of those that a mesh axis runs over, the one named last changes fastest.
Arguments:
- field: bfloat16 [3, 4, 32, 32, 256], P(None, 'face', 'sub'), may hold values from -6 to 6
- dw_kernel: float32 [9, 256], replicated, may hold values from -2 to 2
- dw_bias: float32 [256], replicated, may hold values from -3 to 3
- zonal_kernel: float32 [7, 256], replicated, may hold values from -2 to 2
- zonal_bias: float32 [256], replicated, may hold values from -3 to 3
- norm_gain: float32 [256], replicated, may hold values from 0.1 to 1.9
- w_in: bfloat16 [256, 768], replicated, may hold values from -0.375 to 0.375
- w_out: bfloat16 [768, 256], replicated, may hold values from -0.21875 to 0.21875
- layer_scale: float32 [256], replicated, may hold values from 0.5 to 1.5
Outputs:
- output: bfloat16 [3, 4, 32, 32, 256], P(None, 'face', 'sub')
All inputs are finite; a program needn't handle non-finite values.
Results may differ from a plain program's by a relative error of at most 0.001.
The roundings to bfloat16 on the way count: a program that leaves them out, or rounds other values in their place, can miss the bound.
Values may be sent and summed in bfloat16 or wider, within the bound.
No kernel may reach another device: no remote copies, remote signals or barrier semaphores. Data moves between devices by JAX's collectives and lax.ppermute only.
A program may use at most 64 MiB of HBM per device.

v0:
```python
import jax
import jax.numpy as jnp
from jax import lax
from jax.sharding import PartitionSpec as P

TAPS = 7
DILATION = 4


def from_root(value, axis, root):
    mine = lax.axis_index(axis) == root
    return lax.psum(jnp.where(mine, value, jnp.zeros_like(value)), axis)


def extended_2(block, sides, width, periodic):
    for axis, dim in sides:
        count = lax.axis_size(axis)
        forward = [(i, i + 1) for i in range(count - 1)]
        if periodic:
            forward.append((count - 1, 0))
        backward = [(target, source) for source, target in forward]
        low = lax.ppermute(
            lax.slice_in_dim(block, block.shape[dim] - width, None, axis=dim), axis, forward
        )
        high = lax.ppermute(lax.slice_in_dim(block, 0, width, axis=dim), axis, backward)
        block = jnp.concatenate([low, block, high], axis=dim)
    return block


def cycle_place(facet, column, row_pos, side):
    cycle = (facet + 2) * side - column - row_pos - 1
    along = jnp.where(
        facet == 0,
        column + cycle - side,
        jnp.where((facet == 1) & (cycle < 2 * side), column + cycle - 2 * side, column),
    )
    arc_len = jnp.minimum(jnp.minimum(cycle, side), 4 * side - cycle)
    return (cycle, along, arc_len)


def cycle_cell(cycle, along, side):
    north = (cycle < 2 * side) & (along >= cycle - side)
    middle = jnp.logical_not(north) & (along < 3 * side - cycle)
    facet = jnp.where(north, jnp.int32(0), jnp.where(middle, jnp.int32(1), jnp.int32(2)))
    column = jnp.where(
        north,
        along - cycle + side,
        jnp.where(middle & (cycle < 2 * side), along + 2 * side - cycle, along),
    )
    row_pos = (facet + 2) * side - 1 - cycle - column
    return (facet, column, row_pos)


def spread_rows(face_rows, root):
    return from_root(face_rows, "sub", root)


def take_row(segment_block, permutation):
    return jnp.take(segment_block, permutation, axis=2)


def reorder(values, order):
    return jax.vmap(take_row, in_axes=(1, 0), out_axes=1)(values, order)


def shards(
    field, dw_kernel, dw_bias, zonal_kernel, zonal_bias, norm_gain, w_in, w_out, layer_scale
):
    local_field = field[:, 0]
    rows_here = local_field.shape[1]
    side_cells = local_field.shape[2]
    channels = local_field.shape[3]
    edge_index = side_cells - 1
    sub_count = lax.axis_size("sub")
    quad_total = lax.axis_size("face")
    sub_index = lax.axis_index("sub")
    quad_index = lax.axis_index("face")
    row_start = sub_index * rows_here
    side_pair = jnp.stack([local_field[1, :, 0], local_field[2, :, edge_index]])
    beside_all = extended_2(side_pair, (("face", 0),), 1, True)
    cap_pair = jnp.stack([local_field[0, :, edge_index], local_field[2, :, 0]])
    caps_whole = lax.all_gather(cap_pair, "sub", axis=1, tiled=True)
    top_rows = spread_rows(local_field[:, rows_here - 1], sub_count - 1)
    bottom_rows = spread_rows(local_field[:, 0], 0)
    outgoing = jnp.concatenate(
        [top_rows[0:2], caps_whole[1:2], bottom_rows[2:3], bottom_rows[0:1], caps_whole[0:1]], 0
    )
    rows_around = extended_2(outgoing, (("face", 0),), 3, True)
    left_slice = lax.dynamic_slice_in_dim(rows_around[0], row_start, rows_here, 0)
    right_slice = lax.dynamic_slice_in_dim(rows_around[9], row_start, rows_here, 0)
    face_top = jnp.stack([rows_around[10], top_rows[2], rows_around[11]])
    face_bottom = jnp.stack([rows_around[2], rows_around[1], bottom_rows[1]])
    left_side = jnp.stack([local_field[1, :, edge_index], beside_all[0], left_slice])
    right_side = jnp.stack([right_slice, local_field[0, :, 0], beside_all[3]])
    widened = jnp.concatenate([left_side[:, :, None], local_field, right_side[:, :, None]], 2)
    extended = extended_2(widened, (("sub", 1),), 1, False)
    corner = jnp.zeros((3, 1, channels), local_field.dtype)
    face_top = jnp.concatenate([corner, face_top, corner], 1)
    face_bottom = jnp.concatenate([corner, face_bottom, corner], 1)
    first_row = jnp.where(sub_index == 0, face_top, extended[:, 0])
    final_row = jnp.where(sub_index == sub_count - 1, face_bottom, extended[:, rows_here + 1])
    padded = jnp.concatenate(
        [first_row[:, None], extended[:, 1 : rows_here + 1], final_row[:, None]], 1
    )
    total = jnp.zeros((3, rows_here, side_cells, channels), jnp.float32) + dw_bias
    for i in range(3):
        for j in range(3):
            total = total + dw_kernel[3 * i + j] * padded[
                :, i : i + rows_here, j : j + side_cells
            ].astype(jnp.float32)
    mixed = total.astype(jnp.bfloat16)
    shard_count = quad_total * sub_count
    shard_id = quad_index * sub_count + sub_index
    blocks = side_cells // shard_count
    row_ids = row_start + lax.broadcasted_iota(jnp.int32, (rows_here, shard_count), 0)
    shard_ids = lax.broadcasted_iota(jnp.int32, (rows_here, shard_count), 1)
    order = (-row_ids - 1 - shard_ids) % shard_count
    sending = reorder(mixed.reshape(3, rows_here, blocks, shard_count, channels), order)
    arrived = lax.all_to_all(sending, ("face", "sub"), split_axis=3, concat_axis=3, tiled=True)
    buffer = arrived.reshape(3, rows_here, blocks, quad_total, sub_count, channels)
    shape_out = (3, rows_here, blocks, quad_total, sub_count)
    facet = lax.broadcasted_iota(jnp.int32, shape_out, 0)
    row_local = lax.broadcasted_iota(jnp.int32, shape_out, 1)
    block_ids = lax.broadcasted_iota(jnp.int32, shape_out, 2)
    quad_out = lax.broadcasted_iota(jnp.int32, shape_out, 3)
    sub_source = lax.broadcasted_iota(jnp.int32, shape_out, 4)
    row_pos = sub_source * rows_here + row_local
    residue = (-row_pos - 1 - shard_id) % shard_count
    column = shard_count * block_ids + residue
    cycle, along, arc_len = cycle_place(facet, column, row_pos, side_cells)
    place = quad_out * arc_len + along
    flat = buffer.reshape(-1, channels)
    half = TAPS // 2
    accum = jnp.zeros(shape_out + (channels,), jnp.float32) + zonal_bias
    for k in range(TAPS):
        moved = (place + DILATION * (k - half)) % (4 * arc_len)
        quad_new = moved // arc_len
        along_new = moved % arc_len
        facet_new, column_new, row_new = cycle_cell(cycle, along_new, side_cells)
        index = (
            ((facet_new * rows_here + row_new % rows_here) * blocks + column_new // shard_count)
            * quad_total
            + quad_new
        ) * sub_count + row_new // rows_here
        gathered = jnp.take(flat, index.reshape(-1), axis=0).reshape(shape_out + (channels,))
        accum = accum + zonal_kernel[k] * gathered.astype(jnp.float32)
    zonal = accum.astype(jnp.bfloat16)
    returned = lax.all_to_all(
        zonal.reshape(3, rows_here, blocks, shard_count, channels),
        ("face", "sub"),
        split_axis=3,
        concat_axis=3,
        tiled=True,
    )
    restored = reorder(returned, order).reshape(3, rows_here, side_cells, channels)

    def finish(pair):
        zonal_face, input_face = pair
        values = zonal_face.reshape(-1, channels).astype(jnp.float32)
        mean = jnp.mean(values, -1, keepdims=True)
        spread = jnp.mean(jnp.square(values - mean), -1, keepdims=True)
        normed = ((values - mean) * lax.rsqrt(spread + 1e-06) * norm_gain).astype(jnp.bfloat16)
        hidden = jax.nn.gelu(
            jnp.dot(normed, w_in, preferred_element_type=jnp.float32), approximate=False
        ).astype(jnp.bfloat16)
        branch = jnp.dot(hidden, w_out, preferred_element_type=jnp.float32)
        source = input_face.reshape(-1, channels).astype(jnp.float32)
        result = (source + layer_scale * branch).astype(jnp.bfloat16)
        return result.reshape(rows_here, side_cells, channels)

    output = lax.map(finish, (restored, local_field))
    return output[:, None]


def solution(mesh):
    in_specs = (P(None, "face", "sub", None, None), P(), P(), P(), P(), P(), P(), P(), P())
    out_specs = P(None, "face", "sub", None, None)
    return jax.shard_map(shards, mesh=mesh, in_specs=in_specs, out_specs=out_specs, check_vma=False)
```

profile of v0, /device:TPU:1, one launch (start us, length us, event | category | flops | bytes accessed | tf_op | source)
XLA Modules:
  0.0 143.5 jit_solution(5155847325910490808)
XLA Ops:
  6.5 0.8 fusion.173
  7.4 2.1 %collective-permute-start.1 = (bf16[1,4,256]{2,1,0:T(4,128)(2,1)S(1)}, bf16[1,4,256]{2,1,0:T(4,128)(2,1)S(1)}, u32[]{:S(2)}, u32[]{:S(2)}) collective-permute-start(bf16[1,4,256]{2,1,0:T(4,128)(2,1)S(1)} %bitcast.167), channel_id=1, source_target_pairs={{0,8},{8,16},{16,24},{24,0},{1,9},{9,17},{17,25},{25,1},{2,10},{10... | collective-permute-start | bytes 6152 | tf_op jit(solution)/shard_map/ppermute | solution.py:22
  9.5 1.0 collective-permute-start.3
  10.5 1.5 %fusion.89 = (bf16[3,32,256]{2,1,0:T(8,128)(2,1)}, bf16[3,32,256]{2,1,0:T(8,128)(2,1)}) fusion(bf16[3,4,32,256]{3,2,1,0:T(8,128)(2,1)} %bitcast.133, pred[]{:T(512)S(6)} %eq.77, pred[]{:T(512)S(6)} %eq.78), kind=kLoop, calls=%fused_computation.144 | loop fusion | flops 49152 | bytes 196610 | tf_op jit(solution)/shard_map/jit(_where)/select_n | solution.py:12
  12.3 15.4 %all_gather.3 = bf16[2,32,256]{2,0,1:T(2,128)(2,1)S(1)} all-gather(bf16[2,4,256]{2,0,1:T(2,128)(2,1)S(1)} %copy.188), channel_id=1, replica_groups=mesh['face'=4,'sub'=8] {'sub'}, dimensions={1}, use_global_device_ids=true | all-gather | bytes 36864 | tf_op jit(solution)/shard_map/all_gather | solution.py:82
  27.7 0.7 copy-done.4
  29.1 0.3 compare_and_fusion.7
  29.4 0.9 compare_and_fusion.6
  30.5 33.9 %all-reduce.3.cloned.1.call-done = (bf16[3,32,256]{2,1,0:T(8,128)(2,1)}, bf16[3,32,256]{2,1,0:T(8,128)(2,1)}) async-done(((bf16[3,32,256]{2,1,0:T(8,128)(2,1)}, bf16[3,32,256]{2,1,0:T(8,128)(2,1)}), (bf16[3,32,256]{2,1,0:T(8,128)(2,1)}, bf16[3,32,256]{2,1,0:T(8,128)(2,1)})) %all-reduce.3.cloned.1.call-update) | async-done | bytes 98320 | tf_op jit(solution)/shard_map/psum | solution.py:12
  64.4 0.8 fusion.176
  65.2 1.2 collective-permute-start.2
  66.4 1.7 %collective-permute-start = (bf16[3,32,256]{2,1,0:T(8,128)(2,1)S(1)}, bf16[3,32,256]{2,1,0:T(8,128)(2,1)S(1)}, u32[]{:S(2)}, u32[]{:S(2)}) collective-permute-start(bf16[3,32,256]{2,1,0:T(8,128)(2,1)S(1)} %pad_maximum_fusion.10), channel_id=1, source_target_pairs={{8,0},{16,8},{24,16},{0,24},{9,1},{17,9},{25,17},{1,25},{10,2},{18... | collective-permute-start | bytes 147464 | tf_op jit(solution)/shard_map/ppermute | solution.py:25
  68.1 0.9 collective-permute-done.2
  69.1 0.5 collective-permute-done
  69.8 7.1 %collective-permute-start.4 = (bf16[3,1,34,256]{3,2,1,0:T(8,128)(2,1)S(1)}, bf16[3,1,34,256]{3,2,1,0:T(8,128)(2,1)S(1)}, u32[]{:S(2)}, u32[]{:S(2)}) collective-permute-start(bf16[3,1,34,256]{3,2,1,0:T(8,128)(2,1)S(1)} %get-tuple-element.142), channel_id=1, source_target_pairs={{0,1},{1,2},{2,3},{3,4},{4,5},{5,6},{6,7},{8,9},{9,10},{10,11},{11... | collective-permute-start | bytes 156680 | tf_op jit(solution)/shard_map/ppermute | solution.py:22
  76.9 1.9 %collective-permute-start.5 = (bf16[3,1,34,256]{3,2,1,0:T(8,128)(2,1)S(1)}, bf16[3,1,34,256]{3,2,1,0:T(8,128)(2,1)S(1)}, u32[]{:S(2)}, u32[]{:S(2)}) collective-permute-start(bf16[3,1,34,256]{3,2,1,0:T(8,128)(2,1)S(1)} %get-tuple-element.143), channel_id=1, source_target_pairs={{1,0},{2,1},{3,2},{4,3},{5,4},{6,5},{7,6},{9,8},{10,9},{11,10},{12... | collective-permute-start | bytes 156680 | tf_op jit(solution)/shard_map/ppermute | solution.py:25
  78.9 3.6 %collective-permute-done.5 = bf16[3,1,34,256]{3,2,1,0:T(8,128)(2,1)S(1)} collective-permute-done((bf16[3,1,34,256]{3,2,1,0:T(8,128)(2,1)S(1)}, bf16[3,1,34,256]{3,2,1,0:T(8,128)(2,1)S(1)}, u32[]{:S(2)}, u32[]{:S(2)}) %collective-permute-start.5) | collective-permute-done | bytes 52256 | tf_op jit(solution)/shard_map/ppermute | solution.py:25
  82.7 0.7 copy-done.5
  83.4 0.5 fusion.86
  83.9 0.2 copy.197
  84.1 1.0 gather_fusion
  85.1 0.9 fusion.85
  86.0 3.7 %all-to-all-start = ((bf16[3,4,1,32,256]{4,1,2,0,3:T(4,128)(2,1)}), bf16[3,4,1,32,256]{4,1,2,0,3:T(4,128)(2,1)S(1)}, u32[]{:S(2)}, u32[]{:S(2)}) async-start(bf16[3,4,1,32,256]{4,1,2,0,3:T(4,128)(2,1)} %fusion.85), calls=%async_computation | async-start | bytes 393216 | tf_op jit(solution)/shard_map/all_to_all | solution.py:119
  89.7 0.7 copy-done.3
  90.4 8.6 %all-to-all-done = bf16[3,4,1,32,256]{4,1,2,0,3:T(4,128)(2,1)S(1)} async-done(((bf16[3,4,1,32,256]{4,1,2,0,3:T(4,128)(2,1)}), bf16[3,4,1,32,256]{4,1,2,0,3:T(4,128)(2,1)S(1)}, u32[]{:S(2)}, u32[]{:S(2)}) %all-to-all-start) | async-done | bytes 196640 | tf_op jit(solution)/shard_map/all_to_all | solution.py:119
  99.0 2.1 %gather_fusion.2 = bf16[384,256]{1,0:T(8,128)(2,1)S(1)} fusion(bf16[384,256]{1,0:T(8,128)(2,1)S(1)} %bitcast.125, s32[1024]{0:T(1024)S(1)} %get-tuple-element.200), kind=kCustom, calls=%fused_computation.3.clone | custom fusion | bytes 394752 | tf_op jit(solution)/shard_map/jit(_take)/gather | solution.py:145
  101.1 2.1 %gather_fusion.3 = bf16[384,256]{1,0:T(8,128)(2,1)S(1)} fusion(bf16[384,256]{1,0:T(8,128)(2,1)S(1)} %bitcast.126, s32[1024]{0:T(1024)S(1)} %get-tuple-element.199), kind=kCustom, calls=%fused_computation.4.clone | custom fusion | bytes 394752 | tf_op jit(solution)/shard_map/jit(_take)/gather | solution.py:145
  103.1 2.1 %gather_fusion.4 = bf16[384,256]{1,0:T(8,128)(2,1)S(1)} fusion(bf16[384,256]{1,0:T(8,128)(2,1)S(1)} %bitcast.127, s32[1024]{0:T(1024)S(1)} %get-tuple-element.198), kind=kCustom, calls=%fused_computation.5.clone | custom fusion | bytes 394752 | tf_op jit(solution)/shard_map/jit(_take)/gather | solution.py:145
  105.2 2.1 %gather_fusion.5 = bf16[384,256]{1,0:T(8,128)(2,1)S(1)} fusion(bf16[384,256]{1,0:T(8,128)(2,1)S(1)} %bitcast.128, s32[1024]{0:T(1024)S(1)} %get-tuple-element.197), kind=kCustom, calls=%fused_computation.6.clone | custom fusion | bytes 394752 | tf_op jit(solution)/shard_map/jit(_take)/gather | solution.py:145
  107.3 2.1 %gather_fusion.6 = bf16[384,256]{1,0:T(8,128)(2,1)S(1)} fusion(bf16[384,256]{1,0:T(8,128)(2,1)S(1)} %bitcast.129, s32[1024]{0:T(1024)S(1)} %get-tuple-element.196), kind=kCustom, calls=%fused_computation.7.clone | custom fusion | bytes 394752 | tf_op jit(solution)/shard_map/jit(_take)/gather | solution.py:145
  109.3 2.1 %gather_fusion.1 = bf16[384,256]{1,0:T(8,128)(2,1)S(1)} fusion(bf16[384,256]{1,0:T(8,128)(2,1)S(1)} %bitcast.130, s32[1024]{0:T(1024)S(1)} %pad_clamp_fusion.6), kind=kCustom, calls=%fused_computation.1.clone | custom fusion | bytes 394752 | tf_op jit(solution)/shard_map/jit(_take)/gather | solution.py:145
  111.4 2.1 %gather_fusion.7 = bf16[384,256]{1,0:T(8,128)(2,1)S(1)} fusion(bf16[384,256]{1,0:T(8,128)(2,1)S(1)} %bitcast.131, s32[1024]{0:T(1024)S(1)} %get-tuple-element.195), kind=kCustom, calls=%fused_computation.8.clone | custom fusion | bytes 394752 | tf_op jit(solution)/shard_map/jit(_take)/gather | solution.py:145
  114.4 0.7 copy-done.6
  115.0 0.3 fusion.77
  115.3 0.8 copy.200
  116.2 2.3 %all-to-all-start.1 = ((bf16[3,4,1,32,256]{4,1,2,0,3:T(4,128)(2,1)}), bf16[3,4,1,32,256]{4,1,2,0,3:T(4,128)(2,1)S(1)}, u32[]{:S(2)}, u32[]{:S(2)}) async-start(bf16[3,4,1,32,256]{4,1,2,0,3:T(4,128)(2,1)} %copy.200), calls=%async_computation.1 | async-start | bytes 393216 | tf_op jit(solution)/shard_map/all_to_all | solution.py:148
  118.5 9.1 %all-to-all-done.1 = bf16[3,4,1,32,256]{4,1,2,0,3:T(4,128)(2,1)S(1)} async-done(((bf16[3,4,1,32,256]{4,1,2,0,3:T(4,128)(2,1)}), bf16[3,4,1,32,256]{4,1,2,0,3:T(4,128)(2,1)S(1)}, u32[]{:S(2)}, u32[]{:S(2)}) %all-to-all-start.1) | async-done | bytes 196640 | tf_op jit(solution)/shard_map/all_to_all | solution.py:148
  127.8 1.0 gather_fusion.8
  128.9 0.6 copy-done.2
  129.5 7.2 %while.10 = (s32[]{:T(128)}, bf16[3,4,32,256]{3,2,1,0:T(8,128)(2,1)}, bf16[3,4,32,256]{3,2,1,0:T(8,128)(2,1)S(1)}, f32[256]{0:T(256)S(1)}, bf16[3,4,32,256]{3,2,...) while((s32[]{:T(128)}, ...), condition=%wide.region_5.8_spmd, body=%wide.region_2.7_spmd.sunk | while | flops 107544704 | bytes 1516653 | solution.py:171
  129.6 0.2 multiply_reduce_fusion.2
  130.1 1.1 fusion.196
  131.3 0.6 constant_dynamic-update-slice_fusion.2
  132.0 0.2 multiply_reduce_fusion.2
  132.5 1.1 fusion.196
  133.7 0.6 constant_dynamic-update-slice_fusion.2
  134.9 1.1 fusion.196
  136.1 0.6 constant_dynamic-update-slice_fusion.2
  (105 shorter events, 4.1 us)
Async XLA Ops:
  6.5 57.9 %all-reduce.3.cloned.1.call-start = ((), (), s32[]{:S(2)}) async-start(), calls=%async_computation.2 | async-start | bytes 196608 | tf_op jit(solution)/shard_map/psum | solution.py:12
  7.4 62.2 %collective-permute-start.1 = (bf16[1,4,256]{2,1,0:T(4,128)(2,1)S(1)}, bf16[1,4,256]{2,1,0:T(4,128)(2,1)S(1)}, u32[]{:S(2)}, u32[]{:S(2)}) collective-permute-start(bf16[1,4,256]{2,1,0:T(4,128)(2,1)S(1)} %bitcast.167), channel_id=1, source_target_pairs={{0,8},{8,16},{16,24},{24,0},{1,9},{9,17},{17,25},{25,1},{2,10},{10... | collective-permute-start | bytes 6152 | tf_op jit(solution)/shard_map/ppermute | solution.py:22
  9.5 60.2 %collective-permute-start.3 = (bf16[1,4,256]{2,1,0:T(4,128)(2,1)S(1)}, bf16[1,4,256]{2,1,0:T(4,128)(2,1)S(1)}, u32[]{:S(2)}, u32[]{:S(2)}) collective-permute-start(bf16[1,4,256]{2,1,0:T(4,128)(2,1)S(1)} %bitcast.166), channel_id=1, source_target_pairs={{8,0},{16,8},{24,16},{0,24},{9,1},{17,9},{25,17},{1,25},{10,2},{18... | collective-permute-start | bytes 6152 | tf_op jit(solution)/shard_map/ppermute | solution.py:25
  27.6 0.7 copy-start.4
  65.2 1.3 copy-start.1
  65.2 3.9 %collective-permute-start.2 = (bf16[3,32,256]{2,1,0:T(8,128)(2,1)S(1)}, bf16[3,32,256]{2,1,0:T(8,128)(2,1)S(1)}, u32[]{:S(2)}, u32[]{:S(2)}) collective-permute-start(bf16[3,32,256]{2,1,0:T(8,128)(2,1)S(1)} %pad_maximum_fusion.11), channel_id=1, source_target_pairs={{0,8},{8,16},{16,24},{24,0},{1,9},{9,17},{17,25},{25,1},{2,10},{10... | collective-permute-start | bytes 147464 | tf_op jit(solution)/shard_map/ppermute | solution.py:22
  66.4 3.3 %copy-start = (bf16[3,1,4,32,256]{4,3,2,1,0:T(8,128)(2,1)S(1)}, bf16[3,1,4,32,256]{4,3,2,1,0:T(8,128)(2,1)}, u32[]{:S(2)}) copy-start(bf16[3,1,4,32,256]{4,3,2,1,0:T(8,128)(2,1)} %param.15) | copy-start | bytes 589828
  66.4 3.2 %collective-permute-start = (bf16[3,32,256]{2,1,0:T(8,128)(2,1)S(1)}, bf16[3,32,256]{2,1,0:T(8,128)(2,1)S(1)}, u32[]{:S(2)}, u32[]{:S(2)}) collective-permute-start(bf16[3,32,256]{2,1,0:T(8,128)(2,1)S(1)} %pad_maximum_fusion.10), channel_id=1, source_target_pairs={{8,0},{16,8},{24,16},{0,24},{9,1},{17,9},{25,17},{1,25},{10,2},{18... | collective-permute-start | bytes 147464 | tf_op jit(solution)/shard_map/ppermute | solution.py:25
  69.8 9.1 %collective-permute-start.4 = (bf16[3,1,34,256]{3,2,1,0:T(8,128)(2,1)S(1)}, bf16[3,1,34,256]{3,2,1,0:T(8,128)(2,1)S(1)}, u32[]{:S(2)}, u32[]{:S(2)}) collective-permute-start(bf16[3,1,34,256]{3,2,1,0:T(8,128)(2,1)S(1)} %get-tuple-element.142), channel_id=1, source_target_pairs={{0,1},{1,2},{2,3},{3,4},{4,5},{5,6},{6,7},{8,9},{9,10},{10,11},{11... | collective-permute-start | bytes 156680 | tf_op jit(solution)/shard_map/ppermute | solution.py:22
  76.9 5.5 %collective-permute-start.5 = (bf16[3,1,34,256]{3,2,1,0:T(8,128)(2,1)S(1)}, bf16[3,1,34,256]{3,2,1,0:T(8,128)(2,1)S(1)}, u32[]{:S(2)}, u32[]{:S(2)}) collective-permute-start(bf16[3,1,34,256]{3,2,1,0:T(8,128)(2,1)S(1)} %get-tuple-element.143), channel_id=1, source_target_pairs={{1,0},{2,1},{3,2},{4,3},{5,4},{6,5},{7,6},{9,8},{10,9},{11,10},{12... | collective-permute-start | bytes 156680 | tf_op jit(solution)/shard_map/ppermute | solution.py:25
  82.7 0.7 copy-start.5
  86.0 13.0 %all-to-all-start = ((bf16[3,4,1,32,256]{4,1,2,0,3:T(4,128)(2,1)}), bf16[3,4,1,32,256]{4,1,2,0,3:T(4,128)(2,1)S(1)}, u32[]{:S(2)}, u32[]{:S(2)}) async-start(bf16[3,4,1,32,256]{4,1,2,0,3:T(4,128)(2,1)} %fusion.85), calls=%async_computation | async-start | bytes 393216 | tf_op jit(solution)/shard_map/all_to_all | solution.py:119
  89.7 0.7 copy-start.3
  114.4 0.7 copy-start.6
  116.2 11.5 %all-to-all-start.1 = ((bf16[3,4,1,32,256]{4,1,2,0,3:T(4,128)(2,1)}), bf16[3,4,1,32,256]{4,1,2,0,3:T(4,128)(2,1)S(1)}, u32[]{:S(2)}, u32[]{:S(2)}) async-start(bf16[3,4,1,32,256]{4,1,2,0,3:T(4,128)(2,1)} %copy.200), calls=%async_computation.1 | async-start | bytes 393216 | tf_op jit(solution)/shard_map/all_to_all | solution.py:148
  127.7 1.2 copy-start.7
  127.8 1.2 copy-start.8
  128.8 0.7 copy-start.2
  128.8 0.7 copy-start.9
Sparse Core Ops, SparseCore 0:
  12.1 52.2 all-reduce.2
where the time goes:
time: 144 us
  waiting for transfers between devices  56.6 us (39%)
  local copies, waits for them, and re-layouts  25.9 us (18%)
  starting transfers between devices  21.1 us (15%)
  blocking collectives  15.4 us (11%)
  between operations  13.9 us (10%)
  other arithmetic  6.97 us (5%)
  matrix products  3.45 us (2%)
    psum x1, waiting for transfers between devices, from_root(): return lax.psum(jnp.where(mine, value, jnp.zeros_like(value)), axis)  33.9 us
    all_gather x1, blocking collectives, shards(): caps_whole = lax.all_gather(cap_pair, 'sub', axis=1, tiled=True)  15.4 us
    gather x7, local copies, waits for them, and re-layouts, shards(): jnp.take(flat, index.reshape(-1), axis=0).reshape(shape_out + (channels,))  14.4 us
    ppermute x3, starting transfers between devices, extended_2(): lax.ppermute(lax.slice_in_dim(block, block.shape[dim] - width, None, axis...  10.5 us
    all_to_all x1, waiting for transfers between devices, shards(): lax.all_to_all(zonal.reshape(3, rows_here, blocks, shard_count, channels)...  9.14 us
    all_to_all x1, waiting for transfers between devices, shards(): lax.all_to_all(sending, ('face', 'sub'), split_axis=3, concat_axis=3, til...  8.57 us
    ppermute x3, starting transfers between devices, extended_2(): lax.ppermute(lax.slice_in_dim(block, 0, width, axis=dim), axis, backward)  4.63 us
    ppermute x3, waiting for transfers between devices, extended_2(): lax.ppermute(lax.slice_in_dim(block, 0, width, axis=dim), axis, backward)  4.1 us
  transfers between devices with their start and end apart: 9, of which 6 were waited for; matrix products, arithmetic and copies ran while one was open for 3% of the time, Pallas kernels for 0%

commit v1 on v0

v1 whole, which is shorter than its diff:
```python
import functools

import jax
import jax.numpy as jnp
from jax import lax
from jax.experimental import pallas as pl
from jax.experimental.pallas import tpu as pltpu
from jax.sharding import PartitionSpec as P

TAPS = 7
DILATION = 4
REACH = DILATION * (TAPS // 2)
EPSILON = 1e-06


def fold(count, body, carry, unroll):
    if unroll:
        for i in range(count):
            carry = body(i, carry)
        return carry
    return lax.fori_loop(0, count, body, carry)


def wrap(value, size):
    if isinstance(value, int):
        return value % size
    return lax.rem(value + size, size)


def shift_lanes(values, shift):
    width = values.shape[-1]
    if isinstance(shift, int):
        shift %= width
        if shift == 0:
            return values
    return pltpu.roll(values, shift, values.ndim - 1)


def conv_kernel(quads, subs, side, rows, x_ref, w_ref, o_ref, e_ref, m_ref, ahead_ref, behind_ref):
    width = quads * side
    chans = x_ref.shape[1]
    unroll = width <= 128
    lane = lax.broadcasted_iota(jnp.int32, (chans, width), 1)
    pieces = 3 * rows
    blocks = -(-pieces // quads)

    def load(source):
        return [
            x_ref[source, :, b * width : (b + 1) * width].astype(jnp.float32)
            for b in range(blocks)
        ]

    def to_row(held, face, sub, local):
        piece = face * rows + local
        target = sub * rows + local + (2 - face) * side
        shift = target - (piece % quads) * side
        return shift_lanes(held[piece // quads], wrap(shift, width))

    def plain_row(held, held_before, sub, local):
        y = sub * rows + local
        north = to_row(held, 0, sub, local)
        middle = to_row(held, 1, sub, local)
        south = to_row(held_before, 2, sub, local)
        return jnp.where(lane < y + side, south, jnp.where(lane < y + 2 * side, middle, north))

    last_held = [load(q * subs + subs - 1) for q in range(quads)]
    first_held = [load(q * subs) for q in range(quads)]
    beyond_right, beyond_left = [], []
    for q in range(quads):
        low = plain_row(last_held[q], last_held[q - 1], subs - 1, rows - 1)
        top = plain_row(first_held[q], first_held[q - 1], 0, 0)
        beyond_right.append(shift_lanes(low, 1))
        beyond_left.append(shift_lanes(top, width - 1))

    def build(sub, diagonals):
        diagonals = list(diagonals)
        held = [load(q * subs + sub) for q in range(quads)]
        for q in range(quads):
            for local in range(rows):
                y = sub * rows + local
                row = plain_row(held[q], held[q - 1], sub, local)
                diagonals[2 * q] = jnp.where(lane == y, row, diagonals[2 * q])
                diagonals[2 * q + 1] = jnp.where(
                    lane == y + 3 * side - 1, row, diagonals[2 * q + 1]
                )
                row = jnp.where(lane < y + 3 * side, row, beyond_right[(q + 1) % quads])
                row = jnp.where(lane == wrap(y - 1, width), beyond_left[q - 1], row)
                e_ref[q, side - y] = row
        return tuple(diagonals)

    blank = jnp.zeros((chans, width), jnp.float32)
    diagonals = fold(subs, build, (blank,) * (2 * quads), unroll)
    for q in range(quads):
        after = (q + 1) % quads
        e_ref[q, 0] = jnp.where(
            lane < 3 * side, e_ref[q - 1 if q else quads - 1, side], shift_lanes(diagonals[2 * (q - 1) + 1], 1)
        )
        e_ref[q, side + 1] = jnp.where(
            (lane >= side - 1) & (lane < 3 * side - 1),
            e_ref[after, 1],
            shift_lanes(diagonals[2 * after], width - 1),
        )

    def depthwise(q, u, first=False, last=False):
        below, here, above = e_ref[q, u], e_ref[q, u + 1], e_ref[q, u + 2]
        up_left = shift_lanes(w_ref[0] * above, 2)
        up_right = w_ref[2] * above
        down_left = w_ref[6] * below
        down_right = shift_lanes(w_ref[8] * below, width - 2)
        for k in range(3):
            if first:
                down_left = jnp.where(lane == side - 1 + k * side, 0.0, down_left)
                down_right = jnp.where(lane == 2 * side - 2 + k * side, 0.0, down_right)
            if last:
                up_left = jnp.where(lane == k * side, 0.0, up_left)
                up_right = jnp.where(lane == side - 1 + k * side, 0.0, up_right)
        total = w_ref[9] + w_ref[4] * here
        total = total + (up_right + down_left)
        total = total + shift_lanes(w_ref[1] * above + w_ref[3] * here, 1)
        total = total + shift_lanes(w_ref[5] * here + w_ref[7] * below, width - 1)
        total = total + (up_left + down_right)
        m_ref[q, u] = total.astype(jnp.bfloat16).astype(jnp.float32)

    for q in range(quads):
        depthwise(q, 0, first=True)

        def inner(u, carry, q=q):
            depthwise(q, u + 1)
            return carry

        fold(side - 2, inner, 0, unroll)
        depthwise(q, side - 1, last=True)

    north_cap, south_cap = lane >= 3 * side, lane < side - 1
    arc = jnp.where(north_cap, width - 1 - lane, jnp.where(south_cap, lane + 1, side))
    equator = jnp.logical_not(north_cap | south_cap)
    steps = []
    step = 1
    while step < side:
        steps.insert(0, step)
        step *= 2
    has_step = {step: (arc & step) != 0 for step in steps}

    def sheared(get, head, tail):
        lines = []
        for d in range(side + REACH):
            line = get(0, min(d, side - 1))
            if d < REACH:
                for a in range(1, min(d + 1, REACH)):
                    line = jnp.where(lane == head(a), get(d // a, d % a), line)
            if d >= side:
                for a in range(1, side + REACH - d):
                    place = d - side + a
                    line = jnp.where(
                        lane == tail(a), get(place // a, side - a + place % a), line
                    )
            lines.append(line)
        for step in steps:
            lines = [
                jnp.where(has_step[step], lines[t - step], lines[t]) if t >= step else lines[t]
                for t in range(side + REACH)
            ]
        for t in range(side, side + REACH):
            lines[t] = jnp.where(equator, get(0, t - side), lines[t])
        return lines

    def pole(a):
        return width - 1 - a

    def antipole(a):
        return a - 1

    def extend(q, carry):
        after, before = wrap(q + 1, quads), wrap(q - 1, quads)
        lines = sheared(lambda m, d: m_ref[wrap(after + m, quads), d], pole, antipole)
        for t in range(DILATION, side + REACH):
            if t < side:
                lines[t] = jnp.where(lane >= width - 1 - t, lines[t], m_ref[q, t])
            ahead_ref[q, t - DILATION] = lines[t]
        lines = sheared(
            lambda m, d: m_ref[wrap(before + (-m) % quads, quads), side - 1 - d], antipole, pole
        )
        for t in range(DILATION, side + REACH):
            if t < side:
                lines[t] = jnp.where(lane < t, lines[t], m_ref[q, side - 1 - t])
            behind_ref[q, t - DILATION] = lines[t]
        return carry

    fold(quads, extend, 0, unroll)

    half = TAPS // 2

    def zonal(u, carry):
        for q in range(quads):
            total = w_ref[17] + w_ref[10 + half] * m_ref[q, u]
            for k in range(1, half + 1):
                total = total + w_ref[10 + half + k] * ahead_ref[q, u + DILATION * (k - 1)]
                total = total + w_ref[10 + half - k] * behind_ref[
                    q, side - 1 - u + DILATION * (k - 1)
                ]
            e_ref[q, u] = total
        return carry

    fold(side, zonal, 0, unroll)

    def spread(sub, carry):
        for q in range(quads):
            for b in range(blocks):
                block = None
                for slot in range(quads):
                    piece = b * quads + slot
                    if piece >= pieces:
                        continue
                    face, local = piece // rows, piece % rows
                    y = sub * rows + local
                    strip = q if face < 2 else (q + 1) % quads
                    row = e_ref[strip, side - 1 - y]
                    shift = slot * side - y - (2 - face) * side
                    row = shift_lanes(row, wrap(shift + width, width))
                    block = row if block is None else jnp.where(lane < slot * side, block, row)
                o_ref[q * subs + sub, :, b * width : (b + 1) * width] = block.astype(jnp.bfloat16)
        return carry

    fold(subs, spread, 0, unroll)


def pack_kernel(x_ref, o_ref):
    o_ref[...] = x_ref[...].astype(jnp.float32).T.astype(jnp.bfloat16)


def mlp_kernel(z_ref, x_ref, gain_ref, w_in_ref, w_out_ref, scale_ref, o_ref):
    values = z_ref[...].astype(jnp.float32)
    mean = jnp.mean(values, 0, keepdims=True)
    values = values - mean
    spread = jnp.mean(jnp.square(values), 0, keepdims=True)
    values = values * lax.rsqrt(spread + EPSILON)
    normed = (values.T * gain_ref[...]).astype(jnp.bfloat16)
    inner = jnp.dot(normed, w_in_ref[...], preferred_element_type=jnp.float32)
    hidden = (0.5 * inner * (1.0 + lax.erf(inner * 0.5**0.5))).astype(jnp.bfloat16)
    branch = jnp.dot(hidden, w_out_ref[...], preferred_element_type=jnp.float32)
    o_ref[...] = (x_ref[...].astype(jnp.float32) + scale_ref[...] * branch).astype(jnp.bfloat16)


def shards(
    field, dw_kernel, dw_bias, zonal_kernel, zonal_bias, norm_gain, w_in, w_out, layer_scale
):
    faces, _, rows, side, channels = field.shape
    quads, subs = lax.axis_size("face"), lax.axis_size("sub")
    devices = quads * subs
    share = channels // devices
    cells = faces * rows * side
    width = quads * side
    lanes = -(-cells // width) * width
    chans = -(-share // 8) * 8
    vmem = pl.BlockSpec(memory_space=pltpu.VMEM)
    limit = pltpu.CompilerParams(vmem_limit_bytes=56 * 2**20)

    flat = field.reshape(cells, channels)
    packed = pl.pallas_call(
        pack_kernel,
        out_shape=jax.ShapeDtypeStruct((channels, cells), jnp.bfloat16),
        in_specs=[vmem],
        out_specs=vmem,
        compiler_params=limit,
        name="pack",
    )(flat)
    sent = lax.all_to_all(
        packed.reshape(devices, share, cells), ("face", "sub"), split_axis=0, concat_axis=0, tiled=True
    )
    sent = jnp.pad(sent, ((0, 0), (0, chans - share), (0, lanes - cells)))

    device = lax.axis_index("face") * subs + lax.axis_index("sub")
    weights = jnp.concatenate([dw_kernel, dw_bias[None], zonal_kernel, zonal_bias[None]], 0)
    weights = jnp.pad(weights, ((0, 0), (0, chans - share)))
    weights = lax.dynamic_slice_in_dim(weights, device * share, chans, 1)
    weights = jnp.broadcast_to(weights[:, :, None], weights.shape + (width,))

    extra = side + REACH - DILATION
    zonal = pl.pallas_call(
        functools.partial(conv_kernel, quads, subs, side, rows),
        out_shape=jax.ShapeDtypeStruct((devices, chans, lanes), jnp.bfloat16),
        in_specs=[vmem, vmem],
        out_specs=vmem,
        scratch_shapes=[
            pltpu.VMEM((quads, side + 2, chans, width), jnp.float32),
            pltpu.VMEM((quads, side, chans, width), jnp.float32),
            pltpu.VMEM((quads, extra, chans, width), jnp.float32),
            pltpu.VMEM((quads, extra, chans, width), jnp.float32),
        ],
        compiler_params=limit,
        name="convs",
    )(sent, weights)
    zonal = zonal[:, :share, :cells]
    returned = lax.all_to_all(zonal, ("face", "sub"), split_axis=0, concat_axis=0, tiled=True)

    output = pl.pallas_call(
        mlp_kernel,
        out_shape=jax.ShapeDtypeStruct((cells, channels), jnp.bfloat16),
        in_specs=[vmem] * 6,
        out_specs=vmem,
        compiler_params=limit,
        name="mlp",
    )(returned.reshape(channels, cells), flat, norm_gain[None], w_in, w_out, layer_scale[None])
    return output.reshape(field.shape)


def solution(mesh):
    in_specs = (P(None, "face", "sub", None, None), P(), P(), P(), P(), P(), P(), P(), P())
    out_specs = P(None, "face", "sub", None, None)
    return jax.shard_map(shards, mesh=mesh, in_specs=in_specs, out_specs=out_specs, check_vma=False)
```

time: 144 us -> 37.6 us (0.26)
  waiting for transfers between devices: 56.6 us -> 8.48 us
  local copies, waits for them, and re-layouts: 25.9 us -> 1.43 us
  starting transfers between devices: 21.1 us -> 7.1 us
  between operations: 13.9 us -> 0.05 us
  Pallas kernels: 0 us -> 8.08 us
  other arithmetic: 6.97 us -> 0.08 us
  matrix products: 3.45 us -> 0 us
  blocking collectives: 15.4 us -> 12 us
    psum x1 -> x0, waiting for transfers between devices: 33.9 us -> none  [from_root(): return lax.psum(jnp.where(mine, value, jnp.zeros_like(value)), axis)]
    gather x10 -> x0, local copies, waits for them, and re-layouts: 16.5 us -> none  [the longest x7 14.4 us: shards(): jnp.take(flat, index.reshape(-1), axis=0).reshape(shape_out + (channels,))]
    all_gather x1 -> x0, blocking collectives: 15.4 us -> none  [shards(): caps_whole = lax.all_gather(cap_pair, 'sub', axis=1, tiled=True)]
    ppermute x6 -> x0, starting transfers between devices: 15.1 us -> none  [the longest x3 10.5 us: extended_2(): lax.ppermute(lax.slice_in_dim(block, block.shape[dim] - width, None, axis...]
    all_to_all x0 -> x1, blocking collectives: none -> 12 us  [shards(): lax.all_to_all(zonal, ('face', 'sub'), split_axis=0, concat_axis=0, tiled...]
    all_to_all x2 -> x1, waiting for transfers between devices: 17.7 us -> 8.48 us  [shards(): lax.all_to_all(packed.reshape(devices, share, cells), ('face', 'sub'), sp...]
    pallas_call x0 -> x3, Pallas kernels: none -> 8.08 us  [the longest x1 3.64 us: shards(): pl.pallas_call(functools.partial(conv_kernel, quads, subs, side, rows), o...]
    ppermute x6 -> x0, waiting for transfers between devices: 5.04 us -> none  [the longest x3 4.1 us: extended_2(): lax.ppermute(lax.slice_in_dim(block, 0, width, axis=dim), axis, backward)]
  transfers between devices with their start and end apart: 9 -> 1, of which waited for: 6 -> 1; matrix products, arithmetic and copies ran while one was open for 3% -> 0% of each run, Pallas kernels for 0% -> 0%
where the time goes in v1:
time: 37.6 us; the launch traced here: 37.2 us
  blocking collectives  12 us (32%)
  waiting for transfers between devices  8.48 us (23%)
  Pallas kernels  8.08 us (21%)
  starting transfers between devices  7.1 us (19%)
  local copies, waits for them, and re-layouts  1.43 us (4%)
    all_to_all x1, blocking collectives, shards(): lax.all_to_all(zonal, ('face', 'sub'), split_axis=0, concat_axis=0, tiled...  12 us
    all_to_all x1, waiting for transfers between devices, shards(): lax.all_to_all(packed.reshape(devices, share, cells), ('face', 'sub'), sp...  8.48 us
    all_to_all x1, starting transfers between devices, shards(): lax.all_to_all(packed.reshape(devices, share, cells), ('face', 'sub'), sp...  7.1 us
    pallas_call x1, Pallas kernels, shards(): pl.pallas_call(functools.partial(conv_kernel, quads, subs, side, rows), o...  3.64 us
    pallas_call x1, Pallas kernels, shards(): pl.pallas_call(mlp_kernel, out_shape=jax.ShapeDtypeStruct((cells, channel...  2.69 us
    pallas_call x1, Pallas kernels, shards(): pl.pallas_call(pack_kernel, out_shape=jax.ShapeDtypeStruct((channels, cel...  1.74 us
  transfers between devices with their start and end apart: 1, of which 1 were waited for; matrix products, arithmetic and copies ran while one was open for 0% of the time, Pallas kernels for 0%

profile of v1, /device:TPU:1, one launch (start us, length us, event | category | flops | bytes accessed | tf_op | source)
XLA Modules:
  0.0 37.2 jit_solution(6299981033146778662)
XLA Ops:
  0.0 1.7 %pack.1 = bf16[256,384]{1,0:T(8,128)(2,1)} custom-call(bf16[384,256]{1,0:T(8,128)(2,1)} %bitcast.11), custom_call_target="tpu_custom_call" | custom-call | tf_op jit(solution)/shard_map/pack/pallas_call | solution.py:259
  1.7 7.1 %all-to-all-start = ((bf16[32,8,384]{2,1,0:T(8,128)(2,1)}), bf16[32,8,384]{2,1,0:T(8,128)(2,1)S(1)}, u32[]{:S(2)}, u32[]{:S(2)}) async-start(bf16[32,8,384]{2,1,0:T(8,128)(2,1)} %bitcast.10), calls=%async_computation | async-start | bytes 393216 | tf_op jit(solution)/shard_map/all_to_all | solution.py:267
  8.8 0.0 copy-start.1
  8.9 0.0 copy-start.2
  8.9 0.0 copy-start.4
  8.9 0.0 copy-start.3
  8.9 0.7 %copy-done.1 = f32[9,256]{1,0:T(8,128)S(1)} copy-done((f32[9,256]{1,0:T(8,128)S(1)}, f32[9,256]{1,0:T(8,128)}, u32[]{:S(2)}) %copy-start.1) | copy-done | bytes 9240
  9.6 0.0 copy-done.2
  9.6 0.0 copy-done.4
  9.6 0.0 copy-done.3
  9.6 0.1 fusion.2
  9.7 8.5 %all-to-all-done.x_ref = bf16[32,8,384]{2,1,0:T(8,128)(2,1)S(1)} async-done(((bf16[32,8,384]{2,1,0:T(8,128)(2,1)}), bf16[32,8,384]{2,1,0:T(8,128)(2,1)S(1)}, u32[]{:S(2)}, u32[]{:S(2)}) %all-to-all-start) | async-done | bytes 196640 | tf_op jit(solution)/shard_map/all_to_all | solution.py:267
  18.1 0.0 copy-start
  18.1 0.7 %broadcast_in_dim.20.w_ref = f32[18,8,128]{2,1,0:T(8,128)} broadcast(f32[18,8]{1,0:T(8,128)S(1)} %fusion.2), dimensions={0,1} | broadcast | bytes 74304 | tf_op jit(solution)/shard_map/broadcast_in_dim | solution.py:276
  18.9 0.0 copy-done
  18.9 3.6 %convs.1 = bf16[32,8,384]{2,1,0:T(8,128)(2,1)} custom-call(bf16[32,8,384]{2,1,0:T(8,128)(2,1)} %copy-done, f32[18,8,128]{2,1,0:T(8,128)} %broadcast_in_dim.20.w_ref), custom_call_target="tpu_custom_call" | custom-call | tf_op jit(solution)/shard_map/convs/pallas_call | solution.py:279
  22.5 12.0 %all_to_all.10 = bf16[32,8,384]{2,1,0:T(8,128)(2,1)} all-to-all(bf16[32,8,384]{2,1,0:T(8,128)(2,1)} %convs.1), channel_id=1, replica_groups=mesh['face'=4,'sub'=8] {'face','sub'}, dimensions={0} | all-to-all | bytes 393216 | tf_op jit(solution)/shard_map/all_to_all | solution.py:294
  34.5 2.7 %mlp.1 = bf16[384,256]{1,0:T(8,128)(2,1)} custom-call(bf16[256,384]{1,0:T(8,128)(2,1)} %bitcast.13, bf16[384,256]{1,0:T(8,128)(2,1)} %bitcast.12, f32[1,256]{1,0:T(1,128)} %bitcast.16, bf16[256,768]{1,0:T(8,128)(2,1)} %w_in_ref.1, bf16[768,256]{1,0:T(8,128)(2,1)} %w_out_ref.1, f32[1,256]{1,0:T(1,128)} %bitcast.17), custom_call_target="tpu_custom_call" | custom-call | tf_op jit(solution)/shard_map/mlp/pallas_call | solution.py:296
Async XLA Ops:
  1.7 16.4 %all-to-all-start = ((bf16[32,8,384]{2,1,0:T(8,128)(2,1)}), bf16[32,8,384]{2,1,0:T(8,128)(2,1)S(1)}, u32[]{:S(2)}, u32[]{:S(2)}) async-start(bf16[32,8,384]{2,1,0:T(8,128)(2,1)} %bitcast.10), calls=%async_computation | async-start | bytes 393216 | tf_op jit(solution)/shard_map/all_to_all | solution.py:267
  8.8 0.7 %copy-start.1 = (f32[9,256]{1,0:T(8,128)S(1)}, f32[9,256]{1,0:T(8,128)}, u32[]{:S(2)}) copy-start(f32[9,256]{1,0:T(8,128)} %param.10) | copy-start | bytes 27652
  8.9 0.7 %copy-start.2 = (f32[7,256]{1,0:T(8,128)S(1)}, f32[7,256]{1,0:T(8,128)}, u32[]{:S(2)}) copy-start(f32[7,256]{1,0:T(8,128)} %param.12) | copy-start | bytes 21508
  8.9 0.7 %copy-start.4 = (f32[256]{0:T(256)S(1)}, f32[256]{0:T(256)}, u32[]{:S(2)}) copy-start(f32[256]{0:T(256)} %param.13) | copy-start | bytes 3076
  8.9 0.7 %copy-start.3 = (f32[256]{0:T(256)S(1)}, f32[256]{0:T(256)}, u32[]{:S(2)}) copy-start(f32[256]{0:T(256)} %param.11) | copy-start | bytes 3076
  18.1 0.7 %copy-start = (bf16[32,8,384]{2,1,0:T(8,128)(2,1)}, bf16[32,8,384]{2,1,0:T(8,128)(2,1)S(1)}, u32[]{:S(2)}) copy-start(bf16[32,8,384]{2,1,0:T(8,128)(2,1)S(1)} %all-to-all-done.x_ref) | copy-start | bytes 589828

commit v2 on v1

--- a/solution.py
+++ b/solution.py
@@ -253,7 +253,9 @@
     lanes = -(-cells // width) * width
     chans = -(-share // 8) * 8
     vmem = pl.BlockSpec(memory_space=pltpu.VMEM)
-    limit = pltpu.CompilerParams(vmem_limit_bytes=56 * 2**20)
+    small = pltpu.CompilerParams(vmem_limit_bytes=2**20 + 24 * cells * channels)
+    field_bytes = 4 * devices * chans * lanes
+    large = pltpu.CompilerParams(vmem_limit_bytes=2**20 + 7 * field_bytes)
 
     flat = field.reshape(cells, channels)
     packed = pl.pallas_call(
@@ -261,7 +263,7 @@
         out_shape=jax.ShapeDtypeStruct((channels, cells), jnp.bfloat16),
         in_specs=[vmem],
         out_specs=vmem,
-        compiler_params=limit,
+        compiler_params=small,
         name="pack",
     )(flat)
     sent = lax.all_to_all(
@@ -287,7 +289,7 @@
             pltpu.VMEM((quads, extra, chans, width), jnp.float32),
             pltpu.VMEM((quads, extra, chans, width), jnp.float32),
         ],
-        compiler_params=limit,
+        compiler_params=large,
         name="convs",
     )(sent, weights)
     zonal = zonal[:, :share, :cells]
@@ -298,7 +300,7 @@
         out_shape=jax.ShapeDtypeStruct((cells, channels), jnp.bfloat16),
         in_specs=[vmem] * 6,
         out_specs=vmem,
-        compiler_params=limit,
+        compiler_params=small,
         name="mlp",
     )(returned.reshape(channels, cells), flat, norm_gain[None], w_in, w_out, layer_scale[None])
     return output.reshape(field.shape)

time: 37.6 us -> 34 us (0.904)
  Pallas kernels: 8.08 us -> 4.24 us
  local copies, waits for them, and re-layouts: 1.43 us -> 2.37 us
  blocking collectives: 12 us -> 11.3 us
    pallas_call x1, Pallas kernels: 3.64 us -> 2.02 us  [shards(): pl.pallas_call(functools.partial(conv_kernel, quads, subs, side, rows), o...]
    unnamed x10 -> x20, local copies, waits for them, and re-layouts: 0.7 us -> 2.3 us
    pallas_call x1, Pallas kernels: 2.69 us -> 1.4 us  [shards(): pl.pallas_call(mlp_kernel, out_shape=jax.ShapeDtypeStruct((cells, channel...]
    pallas_call x1, Pallas kernels: 1.74 us -> 0.81 us  [shards(): pl.pallas_call(pack_kernel, out_shape=jax.ShapeDtypeStruct((channels, cel...]
    all_to_all x1, blocking collectives: 12 us -> 11.3 us  [shards(): lax.all_to_all(zonal, ('face', 'sub'), split_axis=0, concat_axis=0, tiled...]
    broadcast_in_dim x1, local copies, waits for them, and re-layouts: 0.73 us -> 0.08 us  [shards(): weights = jnp.broadcast_to(weights[:, :, None], weights.shape + (width,))]
where the time goes in v2:
time: 34 us; the launch traced here: 33.6 us
  blocking collectives  11.3 us (33%)
  waiting for transfers between devices  8.48 us (25%)
  starting transfers between devices  7.1 us (21%)
  Pallas kernels  4.24 us (12%)
  local copies, waits for them, and re-layouts  2.37 us (7%)
    all_to_all x1, blocking collectives, shards(): lax.all_to_all(zonal, ('face', 'sub'), split_axis=0, concat_axis=0, tiled...  11.3 us
    all_to_all x1, waiting for transfers between devices, shards(): lax.all_to_all(packed.reshape(devices, share, cells), ('face', 'sub'), sp...  8.48 us
    all_to_all x1, starting transfers between devices, shards(): lax.all_to_all(packed.reshape(devices, share, cells), ('face', 'sub'), sp...  7.1 us
    unnamed x20, local copies, waits for them, and re-layouts  2.3 us
    pallas_call x1, Pallas kernels, shards(): pl.pallas_call(functools.partial(conv_kernel, quads, subs, side, rows), o...  2.02 us
    pallas_call x1, Pallas kernels, shards(): pl.pallas_call(mlp_kernel, out_shape=jax.ShapeDtypeStruct((cells, channel...  1.4 us
    pallas_call x1, Pallas kernels, shards(): pl.pallas_call(pack_kernel, out_shape=jax.ShapeDtypeStruct((channels, cel...  0.81 us
  transfers between devices with their start and end apart: 1, of which 1 were waited for; matrix products, arithmetic and copies ran while one was open for 0% of the time, Pallas kernels for 0%

profile of v2, /device:TPU:1, one launch (start us, length us, event | category | flops | bytes accessed | tf_op | source)
XLA Modules:
  0.0 33.6 jit_solution(15973959825127077478)
XLA Ops:
  0.0 0.0 copy-start
  0.0 0.9 %copy-done = bf16[3,1,4,32,256]{4,3,2,1,0:T(8,128)(2,1)S(1)} copy-done((bf16[3,1,4,32,256]{4,3,2,1,0:T(8,128)(2,1)S(1)}, bf16[3,1,4,32,256]{4,3,2,1,0:T(8,128)(2,1)}, u32[]{:S(2)}) %copy-start) | copy-done | bytes 196632
  0.9 0.8 %pack.1 = bf16[256,384]{1,0:T(8,128)(2,1)} custom-call(bf16[384,256]{1,0:T(8,128)(2,1)S(1)} %bitcast.10), custom_call_target="tpu_custom_call" | custom-call | tf_op jit(solution)/shard_map/pack/pallas_call | solution.py:261
  1.7 7.1 %all-to-all-start = ((bf16[32,8,384]{2,1,0:T(8,128)(2,1)}), bf16[32,8,384]{2,1,0:T(8,128)(2,1)S(1)}, u32[]{:S(2)}, u32[]{:S(2)}) async-start(bf16[32,8,384]{2,1,0:T(8,128)(2,1)} %bitcast.1), calls=%async_computation | async-start | bytes 393216 | tf_op jit(solution)/shard_map/all_to_all | solution.py:269
  8.8 0.0 copy-start.6
  8.9 0.0 copy-start.7
  8.9 0.0 copy-start.9
  8.9 0.0 copy-start.8
  8.9 0.7 %copy-done.6 = f32[9,256]{1,0:T(8,128)S(1)} copy-done((f32[9,256]{1,0:T(8,128)S(1)}, f32[9,256]{1,0:T(8,128)}, u32[]{:S(2)}) %copy-start.6) | copy-done | bytes 9240
  9.6 0.0 copy-done.7
  9.6 0.0 copy-done.9
  9.6 0.0 copy-done.8
  9.6 0.0 copy-start.3
  9.6 0.1 fusion.2
  9.7 8.5 %all-to-all-done.x_ref = bf16[32,8,384]{2,1,0:T(8,128)(2,1)S(1)} async-done(((bf16[32,8,384]{2,1,0:T(8,128)(2,1)}), bf16[32,8,384]{2,1,0:T(8,128)(2,1)S(1)}, u32[]{:S(2)}, u32[]{:S(2)}) %all-to-all-start) | async-done | bytes 196640 | tf_op jit(solution)/shard_map/all_to_all | solution.py:269
  18.1 0.1 broadcast_in_dim.20.w_ref
  18.2 0.0 copy-start.2
  18.2 2.0 %convs.1 = bf16[32,8,384]{2,1,0:T(8,128)(2,1)S(1)} custom-call(bf16[32,8,384]{2,1,0:T(8,128)(2,1)S(1)} %all-to-all-done.x_ref, f32[18,8,128]{2,1,0:T(8,128)S(1)} %broadcast_in_dim.20.w_ref), custom_call_target="tpu_custom_call" | custom-call | tf_op jit(solution)/shard_map/convs/pallas_call | solution.py:281
  20.3 0.0 copy-start.1
  20.3 0.0 copy-start.5
  20.3 11.3 %all_to_all.10 = bf16[32,8,384]{2,1,0:T(8,128)(2,1)S(1)} all-to-all(bf16[32,8,384]{2,1,0:T(8,128)(2,1)S(1)} %convs.1), channel_id=1, replica_groups=mesh['face'=4,'sub'=8] {'face','sub'}, dimensions={0} | all-to-all | bytes 393216 | tf_op jit(solution)/shard_map/all_to_all | solution.py:296
  31.6 0.0 copy-start.4
  31.6 0.0 copy-done.3
  31.6 0.0 copy-done.2
  31.6 0.0 copy-done.1
  31.6 0.0 copy-done.5
  31.6 0.7 %copy-done.4 = f32[256]{0:T(256)S(1)} copy-done((f32[256]{0:T(256)S(1)}, f32[256]{0:T(256)}, u32[]{:S(2)}) %copy-start.4) | copy-done | bytes 1048
  32.2 1.4 %mlp.1 = bf16[384,256]{1,0:T(8,128)(2,1)} custom-call(bf16[256,384]{1,0:T(8,128)(2,1)S(1)} %bitcast.12, bf16[384,256]{1,0:T(8,128)(2,1)S(1)} %bitcast.11, f32[1,256]{1,0:T(1,128)S(1)} %bitcast.13, bf16[256,768]{1,0:T(8,128)(2,1)S(1)} %copy-done.2, bf16[768,256]{1,0:T(8,128)(2,1)S(1)} %copy-done.3, f32[1,256]{1,0:T(1,128)S(1)} %bitcast.14), custom_call_target="tpu_custom_call" | custom-call | tf_op jit(solution)/shard_map/mlp/pallas_call | solution.py:298
Async XLA Ops:
  0.0 0.9 %copy-start = (bf16[3,1,4,32,256]{4,3,2,1,0:T(8,128)(2,1)S(1)}, bf16[3,1,4,32,256]{4,3,2,1,0:T(8,128)(2,1)}, u32[]{:S(2)}) copy-start(bf16[3,1,4,32,256]{4,3,2,1,0:T(8,128)(2,1)} %param.9) | copy-start | bytes 589828
  1.7 16.4 %all-to-all-start = ((bf16[32,8,384]{2,1,0:T(8,128)(2,1)}), bf16[32,8,384]{2,1,0:T(8,128)(2,1)S(1)}, u32[]{:S(2)}, u32[]{:S(2)}) async-start(bf16[32,8,384]{2,1,0:T(8,128)(2,1)} %bitcast.1), calls=%async_computation | async-start | bytes 393216 | tf_op jit(solution)/shard_map/all_to_all | solution.py:269
  8.8 0.7 %copy-start.6 = (f32[9,256]{1,0:T(8,128)S(1)}, f32[9,256]{1,0:T(8,128)}, u32[]{:S(2)}) copy-start(f32[9,256]{1,0:T(8,128)} %param.10) | copy-start | bytes 27652
  8.9 0.7 %copy-start.7 = (f32[7,256]{1,0:T(8,128)S(1)}, f32[7,256]{1,0:T(8,128)}, u32[]{:S(2)}) copy-start(f32[7,256]{1,0:T(8,128)} %param.12) | copy-start | bytes 21508
  8.9 0.7 %copy-start.9 = (f32[256]{0:T(256)S(1)}, f32[256]{0:T(256)}, u32[]{:S(2)}) copy-start(f32[256]{0:T(256)} %param.13) | copy-start | bytes 3076
  8.9 0.7 %copy-start.8 = (f32[256]{0:T(256)S(1)}, f32[256]{0:T(256)}, u32[]{:S(2)}) copy-start(f32[256]{0:T(256)} %param.11) | copy-start | bytes 3076
  9.6 22.0 %copy-start.3 = (bf16[768,256]{1,0:T(8,128)(2,1)S(1)}, bf16[768,256]{1,0:T(8,128)(2,1)}, u32[]{:S(2)}) copy-start(bf16[768,256]{1,0:T(8,128)(2,1)} %w_out_ref.1) | copy-start | bytes 1179652
  18.2 13.3 %copy-start.2 = (bf16[256,768]{1,0:T(8,128)(2,1)S(1)}, bf16[256,768]{1,0:T(8,128)(2,1)}, u32[]{:S(2)}) copy-start(bf16[256,768]{1,0:T(8,128)(2,1)} %w_in_ref.1) | copy-start | bytes 1179652
  20.3 11.3 %copy-start.1 = (bf16[3,1,4,32,256]{4,3,2,1,0:T(8,128)(2,1)S(1)}, bf16[3,1,4,32,256]{4,3,2,1,0:T(8,128)(2,1)}, u32[]{:S(2)}) copy-start(bf16[3,1,4,32,256]{4,3,2,1,0:T(8,128)(2,1)} %param.9) | copy-start | bytes 589828
  20.3 11.3 %copy-start.5 = (f32[256]{0:T(256)S(1)}, f32[256]{0:T(256)}, u32[]{:S(2)}) copy-start(f32[256]{0:T(256)} %param.17) | copy-start | bytes 3076
  31.6 0.7 %copy-start.4 = (f32[256]{0:T(256)S(1)}, f32[256]{0:T(256)}, u32[]{:S(2)}) copy-start(f32[256]{0:T(256)} %param.14) | copy-start | bytes 3076

commit v3 on v2

--- a/solution.py
+++ b/solution.py
@@ -224,21 +224,66 @@
     fold(subs, spread, 0, unroll)
 
 
-def pack_kernel(x_ref, o_ref):
-    o_ref[...] = x_ref[...].astype(jnp.float32).T.astype(jnp.bfloat16)
-
-
-def mlp_kernel(z_ref, x_ref, gain_ref, w_in_ref, w_out_ref, scale_ref, o_ref):
-    values = z_ref[...].astype(jnp.float32)
-    mean = jnp.mean(values, 0, keepdims=True)
-    values = values - mean
-    spread = jnp.mean(jnp.square(values), 0, keepdims=True)
-    values = values * lax.rsqrt(spread + EPSILON)
-    normed = (values.T * gain_ref[...]).astype(jnp.bfloat16)
-    inner = jnp.dot(normed, w_in_ref[...], preferred_element_type=jnp.float32)
-    hidden = (0.5 * inner * (1.0 + lax.erf(inner * 0.5**0.5))).astype(jnp.bfloat16)
-    branch = jnp.dot(hidden, w_out_ref[...], preferred_element_type=jnp.float32)
-    o_ref[...] = (x_ref[...].astype(jnp.float32) + scale_ref[...] * branch).astype(jnp.bfloat16)
+def pack_kernel(share, fold_axes, *refs):
+    x_hbm, params, o_ref, w_ref, vec_ref = refs[0], refs[1:7], refs[7], refs[8], refs[9]
+    x_vmem, held, columns, table, x_sems, sems = refs[10], refs[11:17], refs[17], refs[18], refs[19], refs[20]
+    parts = x_vmem.shape[0]
+    rows = x_vmem.shape[1]
+    loads = [
+        pltpu.make_async_copy(x_hbm.at[pl.ds(i * rows, rows)], x_vmem.at[i], x_sems.at[i])
+        for i in range(parts)
+    ]
+    small = [
+        pltpu.make_async_copy(source, target, sems.at[i])
+        for i, (source, target) in enumerate(zip(params, held, strict=True))
+    ]
+    for copy in small + loads:
+        copy.start()
+    for copy in small:
+        copy.wait()
+    first = 0
+    for target in held[:4]:
+        table[first : first + target.shape[0], :] = target[...]
+        first += target.shape[0]
+    vec_ref[0:1, :] = held[4][...]
+    vec_ref[1:2, :] = held[5][...]
+    channels = table.shape[1]
+    columns[0:channels, :] = table[...].T
+    device = lax.axis_index(fold_axes[0]) * lax.axis_size(fold_axes[1]) + lax.axis_index(fold_axes[1])
+    start = device * share
+    if share % 8 == 0:
+        start = pl.multiple_of(start, 8)
+    mine = columns[pl.ds(start, w_ref.shape[1]), :]
+    for k in range(w_ref.shape[0]):
+        w_ref[k] = jnp.broadcast_to(mine[:, k : k + 1], w_ref.shape[1:])
+    for i in range(parts):
+        loads[i].wait()
+        o_ref[:, i * rows : (i + 1) * rows] = (
+            x_vmem[i].astype(jnp.float32).T.astype(jnp.bfloat16)
+        )
+
+
+def mlp_kernel(z_ref, x_ref, vec_ref, w_in_ref, w_out_ref, o_hbm, o_vmem, sems):
+    parts, rows = o_vmem.shape[0], o_vmem.shape[1]
+    gain, scale = vec_ref[0:1, :], vec_ref[1:2, :]
+    stores = []
+    for i in range(parts):
+        values = z_ref[:, i * rows : (i + 1) * rows].astype(jnp.float32)
+        mean = jnp.mean(values, 0, keepdims=True)
+        values = values - mean
+        spread = jnp.mean(jnp.square(values), 0, keepdims=True)
+        values = values * lax.rsqrt(spread + EPSILON)
+        normed = (values.T * gain).astype(jnp.bfloat16)
+        inner = jnp.dot(normed, w_in_ref[...], preferred_element_type=jnp.float32)
+        hidden = (0.5 * inner * (1.0 + lax.erf(inner * 0.5**0.5))).astype(jnp.bfloat16)
+        branch = jnp.dot(hidden, w_out_ref[...], preferred_element_type=jnp.float32)
+        source = x_ref[i * rows : (i + 1) * rows, :].astype(jnp.float32)
+        o_vmem[i] = (source + scale * branch).astype(jnp.bfloat16)
+        store = pltpu.make_async_copy(o_vmem.at[i], o_hbm.at[pl.ds(i * rows, rows)], sems.at[i])
+        store.start()
+        stores.append(store)
+    for store in stores:
+        store.wait()
 
 
 def shards(
@@ -258,24 +303,37 @@
     large = pltpu.CompilerParams(vmem_limit_bytes=2**20 + 7 * field_bytes)
 
     flat = field.reshape(cells, channels)
-    packed = pl.pallas_call(
-        pack_kernel,
-        out_shape=jax.ShapeDtypeStruct((channels, cells), jnp.bfloat16),
-        in_specs=[vmem],
-        out_specs=vmem,
+    hbm = pl.BlockSpec(memory_space=pltpu.HBM)
+    part = 128
+    parts = cells // part
+    params = (
+        dw_kernel, dw_bias[None], zonal_kernel, zonal_bias[None], norm_gain[None], layer_scale[None]
+    )
+    taps = sum(p.shape[0] for p in params[:4])
+    packed, weights, vectors = pl.pallas_call(
+        functools.partial(pack_kernel, share, ("face", "sub")),
+        out_shape=(
+            jax.ShapeDtypeStruct((channels, cells), jnp.bfloat16),
+            jax.ShapeDtypeStruct((taps, chans, width), jnp.float32),
+            jax.ShapeDtypeStruct((2, channels), jnp.float32),
+        ),
+        in_specs=[hbm] * 7,
+        out_specs=(vmem, vmem, vmem),
+        scratch_shapes=[pltpu.VMEM((parts, part, channels), jnp.bfloat16)]
+        + [pltpu.VMEM(p.shape, jnp.float32) for p in params]
+        + [
+            pltpu.VMEM((channels + chans, 128), jnp.float32),
+            pltpu.VMEM((128, channels), jnp.float32),
+            pltpu.SemaphoreType.DMA((parts,)),
+            pltpu.SemaphoreType.DMA((len(params),)),
+        ],
         compiler_params=small,
         name="pack",
-    )(flat)
+    )(*(pltpu.with_memory_space_constraint(array, pltpu.HBM) for array in (flat, *params)))
     sent = lax.all_to_all(
         packed.reshape(devices, share, cells), ("face", "sub"), split_axis=0, concat_axis=0, tiled=True
     )
     sent = jnp.pad(sent, ((0, 0), (0, chans - share), (0, lanes - cells)))
-
-    device = lax.axis_index("face") * subs + lax.axis_index("sub")
-    weights = jnp.concatenate([dw_kernel, dw_bias[None], zonal_kernel, zonal_bias[None]], 0)
-    weights = jnp.pad(weights, ((0, 0), (0, chans - share)))
-    weights = lax.dynamic_slice_in_dim(weights, device * share, chans, 1)
-    weights = jnp.broadcast_to(weights[:, :, None], weights.shape + (width,))
 
     extra = side + REACH - DILATION
     zonal = pl.pallas_call(
@@ -298,11 +356,15 @@
     output = pl.pallas_call(
         mlp_kernel,
         out_shape=jax.ShapeDtypeStruct((cells, channels), jnp.bfloat16),
-        in_specs=[vmem] * 6,
-        out_specs=vmem,
+        in_specs=[vmem] * 5,
+        out_specs=hbm,
+        scratch_shapes=[
+            pltpu.VMEM((parts, part, channels), jnp.bfloat16),
+            pltpu.SemaphoreType.DMA((parts,)),
+        ],
         compiler_params=small,
         name="mlp",
-    )(returned.reshape(channels, cells), flat, norm_gain[None], w_in, w_out, layer_scale[None])
+    )(returned.reshape(channels, cells), flat, vectors, w_in, w_out)
     return output.reshape(field.shape)
 
 

time: 34 us -> 32.6 us (0.959)
  blocking collectives: 11.3 us -> 27.5 us
  waiting for transfers between devices: 8.48 us -> 0 us
  starting transfers between devices: 7.1 us -> 0 us
  local copies, waits for them, and re-layouts: 2.37 us -> 0.02 us
  Pallas kernels: 4.24 us -> 4.8 us
    all_to_all x0 -> x1, blocking collectives: none -> 16.2 us  [shards(): lax.all_to_all(packed.reshape(devices, share, cells), ('face', 'sub'), sp...]
    all_to_all x1 -> x0, waiting for transfers between devices: 8.48 us -> none  [shards(): lax.all_to_all(packed.reshape(devices, share, cells), ('face', 'sub'), sp...]
    all_to_all x1 -> x0, starting transfers between devices: 7.1 us -> none  [shards(): lax.all_to_all(packed.reshape(devices, share, cells), ('face', 'sub'), sp...]
    unnamed x20 -> x6, local copies, waits for them, and re-layouts: 2.3 us -> 0.02 us
    pallas_call x1, Pallas kernels: 0.81 us -> 1.42 us  [shards(): pl.pallas_call(functools.partial(pack_kernel, share, ('face', 'sub')), ou...]
  transfers between devices with their start and end apart: 1 -> 0, of which waited for: 1 -> 0; matrix products, arithmetic and copies ran while one was open for 0% -> 0% of each run, Pallas kernels for 0% -> 0%
where the time goes in v3:
time: 32.6 us; the launch traced here: 32.3 us
  blocking collectives  27.5 us (84%)
  Pallas kernels  4.8 us (15%)
    all_to_all x1, blocking collectives, shards(): lax.all_to_all(packed.reshape(devices, share, cells), ('face', 'sub'), sp...  16.2 us
    all_to_all x1, blocking collectives, shards(): lax.all_to_all(zonal, ('face', 'sub'), split_axis=0, concat_axis=0, tiled...  11.3 us
    pallas_call x1, Pallas kernels, shards(): pl.pallas_call(functools.partial(conv_kernel, quads, subs, side, rows), o...  2 us
    pallas_call x1, Pallas kernels, shards(): pl.pallas_call(functools.partial(pack_kernel, share, ('face', 'sub')), ou...  1.42 us
    pallas_call x1, Pallas kernels, shards(): pl.pallas_call(mlp_kernel, out_shape=jax.ShapeDtypeStruct((cells, channel...  1.38 us

profile of v3, /device:TPU:1, one launch (start us, length us, event | category | flops | bytes accessed | tf_op | source)
XLA Modules:
  0.0 32.3 jit_solution(14313463961515956849)
XLA Ops:
  0.0 1.4 %pack.1 = (bf16[256,384]{1,0:T(8,128)(2,1)S(1)}, f32[18,8,128]{2,1,0:T(8,128)S(1)}, f32[2,256]{1,0:T(2,128)S(1)}) custom-call(bf16[384,256]{1,0:T(8,128)(2,1)} %bitcast.10, f32[9,256]{1,0:T(8,128)} %refs_1_.1, f32[1,256]{1,0:T(1,128)} %bitcast.14, f32[7,256]{1,0:T(8,128)} %refs_3_.1, f32[1,256]{1,0:T(1,128)} %bitcast.15, f32[1,256]{1,0:T(1,128)} %bitcast.16, ...), custom_call_target="tpu_custom_call" | custom-call | tf_op jit(solution)/shard_map/pack/pallas_call | solution.py:313
  1.4 0.0 copy-start.2
  1.4 16.2 %all_to_all.10.x_ref = bf16[32,8,384]{2,1,0:T(8,128)(2,1)S(1)} all-to-all(bf16[32,8,384]{2,1,0:T(8,128)(2,1)S(1)} %bitcast.13), channel_id=1, replica_groups=mesh['face'=4,'sub'=8] {'face','sub'}, dimensions={0} | all-to-all | bytes 393216 | tf_op jit(solution)/shard_map/all_to_all | solution.py:333
  17.6 0.0 copy-start.1
  17.6 2.0 %convs.1 = bf16[32,8,384]{2,1,0:T(8,128)(2,1)S(1)} custom-call(bf16[32,8,384]{2,1,0:T(8,128)(2,1)S(1)} %all_to_all.10.x_ref, f32[18,8,128]{2,1,0:T(8,128)S(1)} %get-tuple-element.9.w_ref), custom_call_target="tpu_custom_call" | custom-call | tf_op jit(solution)/shard_map/convs/pallas_call | solution.py:339
  19.6 0.0 copy-start
  19.7 11.3 %all_to_all.11 = bf16[32,8,384]{2,1,0:T(8,128)(2,1)S(1)} all-to-all(bf16[32,8,384]{2,1,0:T(8,128)(2,1)S(1)} %convs.1), channel_id=1, replica_groups=mesh['face'=4,'sub'=8] {'face','sub'}, dimensions={0} | all-to-all | bytes 393216 | tf_op jit(solution)/shard_map/all_to_all | solution.py:354
  30.9 0.0 copy-done.2
  30.9 0.0 copy-done.1
  30.9 0.0 copy-done
  30.9 1.4 %mlp.1 = bf16[384,256]{1,0:T(8,128)(2,1)} custom-call(bf16[256,384]{1,0:T(8,128)(2,1)S(1)} %bitcast.12, bf16[384,256]{1,0:T(8,128)(2,1)S(1)} %bitcast.11, f32[2,256]{1,0:T(2,128)S(1)} %get-tuple-element.10.vec_ref, bf16[256,768]{1,0:T(8,128)(2,1)S(1)} %copy-done.1, bf16[768,256]{1,0:T(8,128)(2,1)S(1)} %copy-done.2), custom_call_target="tpu_custom_call" | custom-call | tf_op jit(solution)/shard_map/mlp/pallas_call | solution.py:356
Async XLA Ops:
  1.4 29.5 %copy-start.2 = (bf16[768,256]{1,0:T(8,128)(2,1)S(1)}, bf16[768,256]{1,0:T(8,128)(2,1)}, u32[]{:S(2)}) copy-start(bf16[768,256]{1,0:T(8,128)(2,1)} %w_out_ref.1) | copy-start | bytes 1179652
  17.6 13.3 %copy-start.1 = (bf16[256,768]{1,0:T(8,128)(2,1)S(1)}, bf16[256,768]{1,0:T(8,128)(2,1)}, u32[]{:S(2)}) copy-start(bf16[256,768]{1,0:T(8,128)(2,1)} %w_in_ref.1) | copy-start | bytes 1179652
  19.6 11.3 %copy-start = (bf16[3,1,4,32,256]{4,3,2,1,0:T(8,128)(2,1)S(1)}, bf16[3,1,4,32,256]{4,3,2,1,0:T(8,128)(2,1)}, u32[]{:S(2)}) copy-start(bf16[3,1,4,32,256]{4,3,2,1,0:T(8,128)(2,1)} %param.9) | copy-start | bytes 589828

commit v4 on v3

--- a/solution.py
+++ b/solution.py
@@ -36,13 +36,22 @@
     return pltpu.roll(values, shift, values.ndim - 1)
 
 
-def conv_kernel(quads, subs, side, rows, x_ref, w_ref, o_ref, e_ref, m_ref, ahead_ref, behind_ref):
+def piece_at(block, slot, faces=3):
+    group, at = divmod(block, faces)
+    first = group * (faces + 1)
+    if slot < faces:
+        return faces - 1 - slot, first + at
+    return faces - 1 - at, first + faces
+
+
+def conv_kernel(
+    quads, subs, side, rows, x_ref, w_ref, o_ref, e_ref, m_ref, ahead_ref, behind_ref, head_ref, tail_ref
+):
     width = quads * side
     chans = x_ref.shape[1]
     unroll = width <= 128
     lane = lax.broadcasted_iota(jnp.int32, (chans, width), 1)
-    pieces = 3 * rows
-    blocks = -(-pieces // quads)
+    blocks = 3 * rows // quads
 
     def load(source):
         return [
@@ -50,17 +59,16 @@
             for b in range(blocks)
         ]
 
-    def to_row(held, face, sub, local):
-        piece = face * rows + local
-        target = sub * rows + local + (2 - face) * side
-        shift = target - (piece % quads) * side
-        return shift_lanes(held[piece // quads], wrap(shift, width))
-
     def plain_row(held, held_before, sub, local):
+        group, at = divmod(local, 4)
         y = sub * rows + local
-        north = to_row(held, 0, sub, local)
-        middle = to_row(held, 1, sub, local)
-        south = to_row(held_before, 2, sub, local)
+        first = 3 * group
+        if at < 3:
+            row = jnp.where(lane < side, held_before[first + at], held[first + at])
+            return shift_lanes(row, y)
+        south = shift_lanes(held_before[first], wrap(y - 3 * side, width))
+        middle = shift_lanes(held[first + 1], wrap(y - 2 * side, width))
+        north = shift_lanes(held[first + 2], wrap(y - side, width))
         return jnp.where(lane < y + side, south, jnp.where(lane < y + 2 * side, middle, north))
 
     last_held = [load(q * subs + subs - 1) for q in range(quads)]
@@ -92,8 +100,9 @@
     diagonals = fold(subs, build, (blank,) * (2 * quads), unroll)
     for q in range(quads):
         after = (q + 1) % quads
+        before = (q - 1) % quads
         e_ref[q, 0] = jnp.where(
-            lane < 3 * side, e_ref[q - 1 if q else quads - 1, side], shift_lanes(diagonals[2 * (q - 1) + 1], 1)
+            lane < 3 * side, e_ref[before, side], shift_lanes(diagonals[2 * before + 1], 1)
         )
         e_ref[q, side + 1] = jnp.where(
             (lane >= side - 1) & (lane < 3 * side - 1),
@@ -132,58 +141,74 @@
         depthwise(q, side - 1, last=True)
 
     north_cap, south_cap = lane >= 3 * side, lane < side - 1
+    northern = lane >= 2 * side
     arc = jnp.where(north_cap, width - 1 - lane, jnp.where(south_cap, lane + 1, side))
     equator = jnp.logical_not(north_cap | south_cap)
     steps = []
     step = 1
     while step < side:
-        steps.insert(0, step)
+        steps.append(step)
         step *= 2
     has_step = {step: (arc & step) != 0 for step in steps}
-
-    def sheared(get, head, tail):
-        lines = []
-        for d in range(side + REACH):
-            line = get(0, min(d, side - 1))
-            if d < REACH:
-                for a in range(1, min(d + 1, REACH)):
-                    line = jnp.where(lane == head(a), get(d // a, d % a), line)
-            if d >= side:
-                for a in range(1, side + REACH - d):
-                    place = d - side + a
-                    line = jnp.where(
-                        lane == tail(a), get(place // a, side - a + place % a), line
-                    )
-            lines.append(line)
-        for step in steps:
-            lines = [
-                jnp.where(has_step[step], lines[t - step], lines[t]) if t >= step else lines[t]
-                for t in range(side + REACH)
-            ]
-        for t in range(side, side + REACH):
-            lines[t] = jnp.where(equator, get(0, t - side), lines[t])
-        return lines
-
-    def pole(a):
-        return width - 1 - a
-
-    def antipole(a):
-        return a - 1
-
-    def extend(q, carry):
-        after, before = wrap(q + 1, quads), wrap(q - 1, quads)
-        lines = sheared(lambda m, d: m_ref[wrap(after + m, quads), d], pole, antipole)
+    for j in range(quads):
+        back = (quads - j) % quads
+        for d in range(REACH):
+            head_ref[j, d] = jnp.where(northern, m_ref[j, d], m_ref[back, side - 1 - d])
+
+        def join(d, carry, j=j, back=back):
+            tail_ref[j, d] = jnp.where(northern, m_ref[back, side - 1 - d], m_ref[j, d])
+            return carry
+
+        fold(side, join, 0, unroll)
+
+    def sheared(inputs):
+        seen = {}
+
+        def line(level, t):
+            if level == len(steps):
+                return inputs.get(t)
+            if (level, t) not in seen:
+                step = steps[level]
+                still, moved = line(level + 1, t), line(level + 1, t - step)
+                if still is not None and moved is not None:
+                    moved = jnp.where(has_step[step], moved, still)
+                seen[level, t] = still if moved is None else moved
+            return seen[level, t]
+
+        return lambda t: line(0, t)
+
+    def extend(j, carry):
+        back = wrap(quads - j, quads)
+        forth_strip, back_strip = wrap(j - 1, quads), wrap(quads + 1 - j, quads)
+        heads, tails = {}, {}
+        for d in range(REACH):
+            line = head_ref[j, d]
+            for a in range(1, min(d + 1, REACH)):
+                line = jnp.where(arc == a, head_ref[wrap(j + d // a, quads), d % a], line)
+            heads[d] = line
+        for d in range(1, side):
+            tails[d] = tail_ref[j, d]
+        for d in range(side, side + REACH - 1):
+            line = None
+            for a in range(1, side + REACH - d):
+                place = d - side + a
+                moved = tail_ref[wrap(j + place // a, quads), side - a + place % a]
+                line = moved if line is None else jnp.where(arc == a, moved, line)
+            tails[d] = line
+        head, tail = sheared(heads), sheared(tails)
         for t in range(DILATION, side + REACH):
+            line = head(t)
             if t < side:
-                lines[t] = jnp.where(lane >= width - 1 - t, lines[t], m_ref[q, t])
-            ahead_ref[q, t - DILATION] = lines[t]
-        lines = sheared(
-            lambda m, d: m_ref[wrap(before + (-m) % quads, quads), side - 1 - d], antipole, pole
-        )
-        for t in range(DILATION, side + REACH):
-            if t < side:
-                lines[t] = jnp.where(lane < t, lines[t], m_ref[q, side - 1 - t])
-            behind_ref[q, t - DILATION] = lines[t]
+                ahead = jnp.where(lane >= width - 1 - t, line, m_ref[forth_strip, t])
+                behind = jnp.where(lane < t, line, m_ref[back_strip, side - 1 - t])
+            else:
+                end = tail(t)
+                ahead = jnp.where(south_cap, end, end if line is None else line)
+                behind = jnp.where(north_cap, end, end if line is None else line)
+                ahead = jnp.where(equator, m_ref[j, t - side], ahead)
+                behind = jnp.where(equator, m_ref[back, 2 * side - 1 - t], behind)
+            ahead_ref[forth_strip, t - DILATION] = ahead
+            behind_ref[back_strip, t - DILATION] = behind
         return carry
 
     fold(quads, extend, 0, unroll)
@@ -204,21 +229,29 @@
     fold(side, zonal, 0, unroll)
 
     def spread(sub, carry):
-        for q in range(quads):
-            for b in range(blocks):
-                block = None
-                for slot in range(quads):
-                    piece = b * quads + slot
-                    if piece >= pieces:
-                        continue
-                    face, local = piece // rows, piece % rows
-                    y = sub * rows + local
-                    strip = q if face < 2 else (q + 1) % quads
-                    row = e_ref[strip, side - 1 - y]
-                    shift = slot * side - y - (2 - face) * side
-                    row = shift_lanes(row, wrap(shift + width, width))
-                    block = row if block is None else jnp.where(lane < slot * side, block, row)
-                o_ref[q * subs + sub, :, b * width : (b + 1) * width] = block.astype(jnp.bfloat16)
+        def row(q, local):
+            return e_ref[q % quads, side - 1 - sub * rows - local]
+
+        for group in range(rows // 4):
+            first = 4 * group
+            y = sub * rows + first
+            aligned = [
+                [shift_lanes(row(q, first + at), wrap(width - y - at, width)) for q in range(quads)]
+                for at in range(3)
+            ]
+            for q in range(quads):
+                for at in range(3):
+                    rest = row(q + 1 if at == 0 else q, first + 3)
+                    rest = shift_lanes(rest, wrap((3 - at) * side - y - 3 + width, width))
+                    block = jnp.where(
+                        lane < side,
+                        aligned[at][(q + 1) % quads],
+                        jnp.where(lane < 3 * side, aligned[at][q], rest),
+                    )
+                    b = 3 * group + at
+                    o_ref[q * subs + sub, :, b * width : (b + 1) * width] = block.astype(
+                        jnp.bfloat16
+                    )
         return carry
 
     fold(subs, spread, 0, unroll)
@@ -227,11 +260,10 @@
 def pack_kernel(share, fold_axes, *refs):
     x_hbm, params, o_ref, w_ref, vec_ref = refs[0], refs[1:7], refs[7], refs[8], refs[9]
     x_vmem, held, columns, table, x_sems, sems = refs[10], refs[11:17], refs[17], refs[18], refs[19], refs[20]
-    parts = x_vmem.shape[0]
-    rows = x_vmem.shape[1]
+    rows, _, side, channels = x_vmem.shape
+    order = [at for at in range(rows) if at % 4 == 3] + [at for at in range(rows) if at % 4 != 3]
     loads = [
-        pltpu.make_async_copy(x_hbm.at[pl.ds(i * rows, rows)], x_vmem.at[i], x_sems.at[i])
-        for i in range(parts)
+        pltpu.make_async_copy(x_hbm.at[:, at], x_vmem.at[at], x_sems.at[at]) for at in order
     ]
     small = [
         pltpu.make_async_copy(source, target, sems.at[i])
@@ -247,7 +279,6 @@
         first += target.shape[0]
     vec_ref[0:1, :] = held[4][...]
     vec_ref[1:2, :] = held[5][...]
-    channels = table.shape[1]
     columns[0:channels, :] = table[...].T
     device = lax.axis_index(fold_axes[0]) * lax.axis_size(fold_axes[1]) + lax.axis_index(fold_axes[1])
     start = device * share
@@ -256,19 +287,22 @@
     mine = columns[pl.ds(start, w_ref.shape[1]), :]
     for k in range(w_ref.shape[0]):
         w_ref[k] = jnp.broadcast_to(mine[:, k : k + 1], w_ref.shape[1:])
-    for i in range(parts):
-        loads[i].wait()
-        o_ref[:, i * rows : (i + 1) * rows] = (
-            x_vmem[i].astype(jnp.float32).T.astype(jnp.bfloat16)
-        )
+    width = 4 * side
+    for block in range(3 * rows // 4):
+        if block % 3 == 0:
+            loads[block // 3].wait()
+        loads[rows // 4 + block].wait()
+        pieces = [x_vmem[local, face] for face, local in (piece_at(block, k) for k in range(4))]
+        o_ref[:, block * width : (block + 1) * width] = jnp.concatenate(pieces, 0).T
 
 
 def mlp_kernel(z_ref, x_ref, vec_ref, w_in_ref, w_out_ref, o_hbm, o_vmem, sems):
-    parts, rows = o_vmem.shape[0], o_vmem.shape[1]
+    parts, slots, side, _ = o_vmem.shape
+    width = slots * side
     gain, scale = vec_ref[0:1, :], vec_ref[1:2, :]
     stores = []
     for i in range(parts):
-        values = z_ref[:, i * rows : (i + 1) * rows].astype(jnp.float32)
+        values = z_ref[:, i * width : (i + 1) * width].astype(jnp.float32)
         mean = jnp.mean(values, 0, keepdims=True)
         values = values - mean
         spread = jnp.mean(jnp.square(values), 0, keepdims=True)
@@ -277,11 +311,22 @@
         inner = jnp.dot(normed, w_in_ref[...], preferred_element_type=jnp.float32)
         hidden = (0.5 * inner * (1.0 + lax.erf(inner * 0.5**0.5))).astype(jnp.bfloat16)
         branch = jnp.dot(hidden, w_out_ref[...], preferred_element_type=jnp.float32)
-        source = x_ref[i * rows : (i + 1) * rows, :].astype(jnp.float32)
-        o_vmem[i] = (source + scale * branch).astype(jnp.bfloat16)
-        store = pltpu.make_async_copy(o_vmem.at[i], o_hbm.at[pl.ds(i * rows, rows)], sems.at[i])
-        store.start()
-        stores.append(store)
+        for k in range(slots):
+            face, local = piece_at(i, k)
+            source = x_ref[face, local].astype(jnp.float32)
+            place = face if k < slots - 1 else k
+            o_vmem[i, place] = (source + scale * branch[k * side : (k + 1) * side]).astype(jnp.bfloat16)
+        line = piece_at(i, 0)[1]
+        face, local = piece_at(i, slots - 1)
+        for at, (source, target) in enumerate(
+            (
+                (o_vmem.at[i, pl.ds(0, slots - 1)], o_hbm.at[:, line]),
+                (o_vmem.at[i, slots - 1], o_hbm.at[face, local]),
+            )
+        ):
+            store = pltpu.make_async_copy(source, target, sems.at[2 * i + at])
+            store.start()
+            stores.append(store)
     for store in stores:
         store.wait()
 
@@ -300,12 +345,10 @@
     vmem = pl.BlockSpec(memory_space=pltpu.VMEM)
     small = pltpu.CompilerParams(vmem_limit_bytes=2**20 + 24 * cells * channels)
     field_bytes = 4 * devices * chans * lanes
-    large = pltpu.CompilerParams(vmem_limit_bytes=2**20 + 7 * field_bytes)
-
-    flat = field.reshape(cells, channels)
+    large = pltpu.CompilerParams(vmem_limit_bytes=2**20 + 9 * field_bytes)
+
+    local = field.reshape(faces, rows, side, channels)
     hbm = pl.BlockSpec(memory_space=pltpu.HBM)
-    part = 128
-    parts = cells // part
     params = (
         dw_kernel, dw_bias[None], zonal_kernel, zonal_bias[None], norm_gain[None], layer_scale[None]
     )
@@ -319,17 +362,17 @@
         ),
         in_specs=[hbm] * 7,
         out_specs=(vmem, vmem, vmem),
-        scratch_shapes=[pltpu.VMEM((parts, part, channels), jnp.bfloat16)]
+        scratch_shapes=[pltpu.VMEM((rows, faces, side, channels), jnp.bfloat16)]
         + [pltpu.VMEM(p.shape, jnp.float32) for p in params]
         + [
             pltpu.VMEM((channels + chans, 128), jnp.float32),
             pltpu.VMEM((128, channels), jnp.float32),
-            pltpu.SemaphoreType.DMA((parts,)),
+            pltpu.SemaphoreType.DMA((rows,)),
             pltpu.SemaphoreType.DMA((len(params),)),
         ],
         compiler_params=small,
         name="pack",
-    )(*(pltpu.with_memory_space_constraint(array, pltpu.HBM) for array in (flat, *params)))
+    )(*(pltpu.with_memory_space_constraint(array, pltpu.HBM) for array in (local, *params)))
     sent = lax.all_to_all(
         packed.reshape(devices, share, cells), ("face", "sub"), split_axis=0, concat_axis=0, tiled=True
     )
@@ -346,6 +389,8 @@
             pltpu.VMEM((quads, side, chans, width), jnp.float32),
             pltpu.VMEM((quads, extra, chans, width), jnp.float32),
             pltpu.VMEM((quads, extra, chans, width), jnp.float32),
+            pltpu.VMEM((quads, REACH, chans, width), jnp.float32),
+            pltpu.VMEM((quads, side, chans, width), jnp.float32),
         ],
         compiler_params=large,
         name="convs",
@@ -355,16 +400,16 @@
 
     output = pl.pallas_call(
         mlp_kernel,
-        out_shape=jax.ShapeDtypeStruct((cells, channels), jnp.bfloat16),
+        out_shape=jax.ShapeDtypeStruct(local.shape, jnp.bfloat16),
         in_specs=[vmem] * 5,
         out_specs=hbm,
         scratch_shapes=[
-            pltpu.VMEM((parts, part, channels), jnp.bfloat16),
-            pltpu.SemaphoreType.DMA((parts,)),
+            pltpu.VMEM((cells // width, quads, side, channels), jnp.bfloat16),
+            pltpu.SemaphoreType.DMA((2 * cells // width,)),
         ],
         compiler_params=small,
         name="mlp",
-    )(returned.reshape(channels, cells), flat, vectors, w_in, w_out)
+    )(returned.reshape(channels, cells), local, vectors, w_in, w_out)
     return output.reshape(field.shape)
 
 

time: 32.6 us -> 32 us (0.982)
  Pallas kernels: 4.8 us -> 4.19 us
    pallas_call x1, Pallas kernels: 2 us -> 1.45 us  [shards(): pl.pallas_call(functools.partial(conv_kernel, quads, subs, side, rows), o...]
where the time goes in v4:
time: 32 us; the launch traced here: 31.7 us
  blocking collectives  27.5 us (86%)
  Pallas kernels  4.19 us (13%)
    all_to_all x1, blocking collectives, shards(): lax.all_to_all(packed.reshape(devices, share, cells), ('face', 'sub'), sp...  16.2 us
    all_to_all x1, blocking collectives, shards(): lax.all_to_all(zonal, ('face', 'sub'), split_axis=0, concat_axis=0, tiled...  11.3 us
    pallas_call x1, Pallas kernels, shards(): pl.pallas_call(functools.partial(conv_kernel, quads, subs, side, rows), o...  1.45 us
    pallas_call x1, Pallas kernels, shards(): pl.pallas_call(mlp_kernel, out_shape=jax.ShapeDtypeStruct(local.shape, jn...  1.4 us
    pallas_call x1, Pallas kernels, shards(): pl.pallas_call(functools.partial(pack_kernel, share, ('face', 'sub')), ou...  1.34 us

profile of v4, /device:TPU:1, one launch (start us, length us, event | category | flops | bytes accessed | tf_op | source)
XLA Modules:
  0.0 31.7 jit_solution(11946607747959289953)
XLA Ops:
  0.0 1.3 %pack.1 = (bf16[256,384]{1,0:T(8,128)(2,1)S(1)}, f32[18,8,128]{2,1,0:T(8,128)S(1)}, f32[2,256]{1,0:T(2,128)S(1)}) custom-call(bf16[3,4,32,256]{3,2,1,0:T(8,128)(2,1)} %bitcast.10, f32[9,256]{1,0:T(8,128)} %refs_1_.1, f32[1,256]{1,0:T(1,128)} %bitcast.14, f32[7,256]{1,0:T(8,128)} %refs_3_.1, f32[1,256]{1,0:T(1,128)} %bitcast.15, f32[1,256]{1,0:T(1,128)} %bitcast.16, ...), custom_call_target="tpu_custom_call" | custom-call | tf_op jit(solution)/shard_map/pack/pallas_call | solution.py:356
  1.3 0.0 copy-start.2
  1.4 16.2 %all_to_all.10.x_ref = bf16[32,8,384]{2,1,0:T(8,128)(2,1)S(1)} all-to-all(bf16[32,8,384]{2,1,0:T(8,128)(2,1)S(1)} %bitcast.13), channel_id=1, replica_groups=mesh['face'=4,'sub'=8] {'face','sub'}, dimensions={0} | all-to-all | bytes 393216 | tf_op jit(solution)/shard_map/all_to_all | solution.py:376
  17.6 0.0 copy-start.1
  17.6 1.4 %convs.1 = bf16[32,8,384]{2,1,0:T(8,128)(2,1)S(1)} custom-call(bf16[32,8,384]{2,1,0:T(8,128)(2,1)S(1)} %all_to_all.10.x_ref, f32[18,8,128]{2,1,0:T(8,128)S(1)} %get-tuple-element.9.w_ref), custom_call_target="tpu_custom_call" | custom-call | tf_op jit(solution)/shard_map/convs/pallas_call | solution.py:382
  19.0 0.0 copy-start
  19.0 11.3 %all_to_all.11 = bf16[32,8,384]{2,1,0:T(8,128)(2,1)S(1)} all-to-all(bf16[32,8,384]{2,1,0:T(8,128)(2,1)S(1)} %convs.1), channel_id=1, replica_groups=mesh['face'=4,'sub'=8] {'face','sub'}, dimensions={0} | all-to-all | bytes 393216 | tf_op jit(solution)/shard_map/all_to_all | solution.py:399
  30.3 0.0 copy-done.2
  30.3 0.0 copy-done.1
  30.3 0.0 copy-done
  30.3 1.4 %mlp.1 = bf16[3,4,32,256]{3,2,1,0:T(8,128)(2,1)} custom-call(bf16[256,384]{1,0:T(8,128)(2,1)S(1)} %bitcast.12, bf16[3,4,32,256]{3,2,1,0:T(8,128)(2,1)S(1)} %bitcast.11, f32[2,256]{1,0:T(2,128)S(1)} %get-tuple-element.10.vec_ref, bf16[256,768]{1,0:T(8,128)(2,1)S(1)} %copy-done.1, bf16[768,256]{1,0:T(8,128)(2,1)S(1)} %copy-done.2), custom_call_target="tpu_custom_call" | custom-call | tf_op jit(solution)/shard_map/mlp/pallas_call | solution.py:401
Async XLA Ops:
  1.3 29.0 %copy-start.2 = (bf16[768,256]{1,0:T(8,128)(2,1)S(1)}, bf16[768,256]{1,0:T(8,128)(2,1)}, u32[]{:S(2)}) copy-start(bf16[768,256]{1,0:T(8,128)(2,1)} %w_out_ref.1) | copy-start | bytes 1179652
  17.6 12.8 %copy-start.1 = (bf16[256,768]{1,0:T(8,128)(2,1)S(1)}, bf16[256,768]{1,0:T(8,128)(2,1)}, u32[]{:S(2)}) copy-start(bf16[256,768]{1,0:T(8,128)(2,1)} %w_in_ref.1) | copy-start | bytes 1179652
  19.0 11.3 %copy-start = (bf16[3,1,4,32,256]{4,3,2,1,0:T(8,128)(2,1)S(1)}, bf16[3,1,4,32,256]{4,3,2,1,0:T(8,128)(2,1)}, u32[]{:S(2)}) copy-start(bf16[3,1,4,32,256]{4,3,2,1,0:T(8,128)(2,1)} %param.9) | copy-start | bytes 589828

commit v5 on v4

--- a/solution.py
+++ b/solution.py
@@ -45,8 +45,10 @@
 
 
 def conv_kernel(
-    quads, subs, side, rows, x_ref, w_ref, o_ref, e_ref, m_ref, ahead_ref, behind_ref, head_ref, tail_ref
+    quads, subs, side, rows, share, axes, x_ref, dw_ref, dw_bias_ref, zonal_ref, zonal_bias_ref, o_ref,
+    e_ref, m_ref, ahead_ref, behind_ref, head_ref, tail_ref, columns, table, w_ref
 ):
+    lay_out(share, axes, (dw_ref, dw_bias_ref, zonal_ref, zonal_bias_ref), columns, table, w_ref)
     width = quads * side
     chans = x_ref.shape[1]
     unroll = width <= 128
@@ -87,12 +89,12 @@
             for local in range(rows):
                 y = sub * rows + local
                 row = plain_row(held[q], held[q - 1], sub, local)
-                diagonals[2 * q] = jnp.where(lane == y, row, diagonals[2 * q])
+                diagonals[2 * q] = jnp.where(lane < y, diagonals[2 * q], row)
                 diagonals[2 * q + 1] = jnp.where(
-                    lane == y + 3 * side - 1, row, diagonals[2 * q + 1]
+                    lane < y + 3 * side - 1, diagonals[2 * q + 1], row
                 )
                 row = jnp.where(lane < y + 3 * side, row, beyond_right[(q + 1) % quads])
-                row = jnp.where(lane == wrap(y - 1, width), beyond_left[q - 1], row)
+                row = jnp.where(lane == wrap(y - 1, width), beyond_left[q - 1], row) if not isinstance(y, int) or y == 0 else jnp.where(lane < y, beyond_left[q - 1], row)
                 e_ref[q, side - y] = row
         return tuple(diagonals)
 
@@ -112,10 +114,10 @@
 
     def depthwise(q, u, first=False, last=False):
         below, here, above = e_ref[q, u], e_ref[q, u + 1], e_ref[q, u + 2]
-        up_left = shift_lanes(w_ref[0] * above, 2)
+        up_left = w_ref[0] * shift_lanes(above, 2)
         up_right = w_ref[2] * above
         down_left = w_ref[6] * below
-        down_right = shift_lanes(w_ref[8] * below, width - 2)
+        down_right = w_ref[8] * shift_lanes(below, width - 2)
         for k in range(3):
             if first:
                 down_left = jnp.where(lane == side - 1 + k * side, 0.0, down_left)
@@ -125,8 +127,8 @@
                 up_right = jnp.where(lane == side - 1 + k * side, 0.0, up_right)
         total = w_ref[9] + w_ref[4] * here
         total = total + (up_right + down_left)
-        total = total + shift_lanes(w_ref[1] * above + w_ref[3] * here, 1)
-        total = total + shift_lanes(w_ref[5] * here + w_ref[7] * below, width - 1)
+        total = total + (w_ref[1] * shift_lanes(above, 1) + w_ref[3] * shift_lanes(here, 1))
+        total = total + (w_ref[5] * shift_lanes(here, width - 1) + w_ref[7] * shift_lanes(below, width - 1))
         total = total + (up_left + down_right)
         m_ref[q, u] = total.astype(jnp.bfloat16).astype(jnp.float32)
 
@@ -215,22 +217,21 @@
 
     half = TAPS // 2
 
-    def zonal(u, carry):
-        for q in range(quads):
-            total = w_ref[17] + w_ref[10 + half] * m_ref[q, u]
-            for k in range(1, half + 1):
-                total = total + w_ref[10 + half + k] * ahead_ref[q, u + DILATION * (k - 1)]
-                total = total + w_ref[10 + half - k] * behind_ref[
-                    q, side - 1 - u + DILATION * (k - 1)
-                ]
-            e_ref[q, u] = total
-        return carry
-
-    fold(side, zonal, 0, unroll)
+    def zonal(q, u):
+        total = w_ref[17] + w_ref[10 + half] * m_ref[q, u]
+        for k in range(1, half + 1):
+            total = total + w_ref[10 + half + k] * ahead_ref[q, u + DILATION * (k - 1)]
+            total = total + w_ref[10 + half - k] * behind_ref[q, side - 1 - u + DILATION * (k - 1)]
+        return total
 
     def spread(sub, carry):
+        seen = {}
+
         def row(q, local):
-            return e_ref[q % quads, side - 1 - sub * rows - local]
+            q %= quads
+            if (q, local) not in seen:
+                seen[q, local] = zonal(q, side - 1 - sub * rows - local)
+            return seen[q, local]
 
         for group in range(rows // 4):
             first = 4 * group
@@ -257,9 +258,23 @@
     fold(subs, spread, 0, unroll)
 
 
-def pack_kernel(share, fold_axes, *refs):
-    x_hbm, params, o_ref, w_ref, vec_ref = refs[0], refs[1:7], refs[7], refs[8], refs[9]
-    x_vmem, held, columns, table, x_sems, sems = refs[10], refs[11:17], refs[17], refs[18], refs[19], refs[20]
+def lay_out(share, axes, params, columns, table, w_ref):
+    first = 0
+    for source in params:
+        table[first : first + source.shape[0], :] = source[...]
+        first += source.shape[0]
+    columns[0 : table.shape[1], :] = table[...].T
+    device = lax.axis_index(axes[0]) * lax.axis_size(axes[1]) + lax.axis_index(axes[1])
+    start = device * share
+    if share % 8 == 0:
+        start = pl.multiple_of(start, 8)
+    mine = columns[pl.ds(start, w_ref.shape[1]), :]
+    for k in range(w_ref.shape[0]):
+        w_ref[k] = jnp.broadcast_to(mine[:, k : k + 1], w_ref.shape[1:])
+
+
+def pack_kernel(x_hbm, *refs):
+    params, o_ref, held, x_vmem, x_sems, sems = refs[:6], refs[6], refs[7:13], refs[13], refs[14], refs[15]
     rows, _, side, channels = x_vmem.shape
     order = [at for at in range(rows) if at % 4 == 3] + [at for at in range(rows) if at % 4 != 3]
     loads = [
@@ -271,35 +286,18 @@
     ]
     for copy in small + loads:
         copy.start()
-    for copy in small:
+    for copy in small + loads:
         copy.wait()
-    first = 0
-    for target in held[:4]:
-        table[first : first + target.shape[0], :] = target[...]
-        first += target.shape[0]
-    vec_ref[0:1, :] = held[4][...]
-    vec_ref[1:2, :] = held[5][...]
-    columns[0:channels, :] = table[...].T
-    device = lax.axis_index(fold_axes[0]) * lax.axis_size(fold_axes[1]) + lax.axis_index(fold_axes[1])
-    start = device * share
-    if share % 8 == 0:
-        start = pl.multiple_of(start, 8)
-    mine = columns[pl.ds(start, w_ref.shape[1]), :]
-    for k in range(w_ref.shape[0]):
-        w_ref[k] = jnp.broadcast_to(mine[:, k : k + 1], w_ref.shape[1:])
     width = 4 * side
     for block in range(3 * rows // 4):
-        if block % 3 == 0:
-            loads[block // 3].wait()
-        loads[rows // 4 + block].wait()
         pieces = [x_vmem[local, face] for face, local in (piece_at(block, k) for k in range(4))]
         o_ref[:, block * width : (block + 1) * width] = jnp.concatenate(pieces, 0).T
 
 
-def mlp_kernel(z_ref, x_ref, vec_ref, w_in_ref, w_out_ref, o_hbm, o_vmem, sems):
+def mlp_kernel(z_ref, x_ref, gain_ref, scale_ref, w_in_ref, w_out_ref, o_hbm, o_vmem, sems):
     parts, slots, side, _ = o_vmem.shape
     width = slots * side
-    gain, scale = vec_ref[0:1, :], vec_ref[1:2, :]
+    gain, scale = gain_ref[...], scale_ref[...]
     stores = []
     for i in range(parts):
         values = z_ref[:, i * width : (i + 1) * width].astype(jnp.float32)
@@ -353,20 +351,16 @@
         dw_kernel, dw_bias[None], zonal_kernel, zonal_bias[None], norm_gain[None], layer_scale[None]
     )
     taps = sum(p.shape[0] for p in params[:4])
-    packed, weights, vectors = pl.pallas_call(
-        functools.partial(pack_kernel, share, ("face", "sub")),
+    packed, *params = pl.pallas_call(
+        pack_kernel,
         out_shape=(
             jax.ShapeDtypeStruct((channels, cells), jnp.bfloat16),
-            jax.ShapeDtypeStruct((taps, chans, width), jnp.float32),
-            jax.ShapeDtypeStruct((2, channels), jnp.float32),
+            *(jax.ShapeDtypeStruct(p.shape, jnp.float32) for p in params),
         ),
         in_specs=[hbm] * 7,
-        out_specs=(vmem, vmem, vmem),
-        scratch_shapes=[pltpu.VMEM((rows, faces, side, channels), jnp.bfloat16)]
-        + [pltpu.VMEM(p.shape, jnp.float32) for p in params]
-        + [
-            pltpu.VMEM((channels + chans, 128), jnp.float32),
-            pltpu.VMEM((128, channels), jnp.float32),
+        out_specs=(vmem,) * 7,
+        scratch_shapes=[
+            pltpu.VMEM((rows, faces, side, channels), jnp.bfloat16),
             pltpu.SemaphoreType.DMA((rows,)),
             pltpu.SemaphoreType.DMA((len(params),)),
         ],
@@ -380,9 +374,9 @@
 
     extra = side + REACH - DILATION
     zonal = pl.pallas_call(
-        functools.partial(conv_kernel, quads, subs, side, rows),
+        functools.partial(conv_kernel, quads, subs, side, rows, share, ("face", "sub")),
         out_shape=jax.ShapeDtypeStruct((devices, chans, lanes), jnp.bfloat16),
-        in_specs=[vmem, vmem],
+        in_specs=[vmem] * 5,
         out_specs=vmem,
         scratch_shapes=[
             pltpu.VMEM((quads, side + 2, chans, width), jnp.float32),
@@ -391,17 +385,20 @@
             pltpu.VMEM((quads, extra, chans, width), jnp.float32),
             pltpu.VMEM((quads, REACH, chans, width), jnp.float32),
             pltpu.VMEM((quads, side, chans, width), jnp.float32),
+            pltpu.VMEM((channels + chans, 128), jnp.float32),
+            pltpu.VMEM((128, channels), jnp.float32),
+            pltpu.VMEM((taps, chans, width), jnp.float32),
         ],
         compiler_params=large,
         name="convs",
-    )(sent, weights)
+    )(sent, *params[:4])
     zonal = zonal[:, :share, :cells]
     returned = lax.all_to_all(zonal, ("face", "sub"), split_axis=0, concat_axis=0, tiled=True)
 
     output = pl.pallas_call(
         mlp_kernel,
         out_shape=jax.ShapeDtypeStruct(local.shape, jnp.bfloat16),
-        in_specs=[vmem] * 5,
+        in_specs=[vmem] * 6,
         out_specs=hbm,
         scratch_shapes=[
             pltpu.VMEM((cells // width, quads, side, channels), jnp.bfloat16),
@@ -409,7 +406,7 @@
         ],
         compiler_params=small,
         name="mlp",
-    )(returned.reshape(channels, cells), local, vectors, w_in, w_out)
+    )(returned.reshape(channels, cells), local, *params[4:], w_in, w_out)
     return output.reshape(field.shape)
 
 

time: 32 us -> 31.8 us (level)
  no operation moved by 1% of the time
where the time goes in v5:
time: 31.8 us; the launch traced here: 31.6 us
  blocking collectives  27.5 us (86%)
  Pallas kernels  4.04 us (13%)
    all_to_all x1, blocking collectives, shards(): lax.all_to_all(packed.reshape(devices, share, cells), ('face', 'sub'), sp...  16.2 us
    all_to_all x1, blocking collectives, shards(): lax.all_to_all(zonal, ('face', 'sub'), split_axis=0, concat_axis=0, tiled...  11.3 us
    pallas_call x1, Pallas kernels, shards(): pl.pallas_call(functools.partial(conv_kernel, quads, subs, side, rows, sh...  1.49 us
    pallas_call x1, Pallas kernels, shards(): pl.pallas_call(mlp_kernel, out_shape=jax.ShapeDtypeStruct(local.shape, jn...  1.4 us
    pallas_call x1, Pallas kernels, shards(): pl.pallas_call(pack_kernel, out_shape=(jax.ShapeDtypeStruct((channels, ce...  1.15 us

profile of v5, /device:TPU:1, one launch (start us, length us, event | category | flops | bytes accessed | tf_op | source)
XLA Modules:
  0.0 31.6 jit_solution(4802337898315638090)
XLA Ops:
  0.0 1.1 %pack.1 = (bf16[256,384]{1,0:T(8,128)(2,1)S(1)}, f32[9,256]{1,0:T(8,128)S(1)}, f32[1,256]{1,0:T(1,128)S(1)}, f32[7,256]{1,0:T(8,128)S(1)}, f32[1,256]{1,0:T(1,12...) custom-call(bf16[3,4,32,256]{3,2,1,0:T(8,128)(2,1)} %bitcast.10, f32[9,256]{1,0:T(8,128)} %refs_0_.1, ...), custom_call_target="tpu_custom_call" | custom-call | tf_op jit(solution)/shard_map/pack/pallas_call | solution.py:354
  1.2 0.0 copy-start.2
  1.2 16.2 %all_to_all.10.x_ref = bf16[32,8,384]{2,1,0:T(8,128)(2,1)S(1)} all-to-all(bf16[32,8,384]{2,1,0:T(8,128)(2,1)S(1)} %bitcast.13), channel_id=1, replica_groups=mesh['face'=4,'sub'=8] {'face','sub'}, dimensions={0} | all-to-all | bytes 393216 | tf_op jit(solution)/shard_map/all_to_all | solution.py:370
  17.4 0.0 copy-start.1
  17.4 1.5 %convs.1 = bf16[32,8,384]{2,1,0:T(8,128)(2,1)S(1)} custom-call(bf16[32,8,384]{2,1,0:T(8,128)(2,1)S(1)} %all_to_all.10.x_ref, f32[9,256]{1,0:T(8,128)S(1)} %get-tuple-element.13.dw_ref, f32[1,256]{1,0:T(1,128)S(1)} %get-tuple-element.14.dw_bias_ref, f32[7,256]{1,0:T(8,128)S(1)} %get-tuple-element.15.zonal_ref, f32[1,256]{1,0:T(1,128)S(1)} %get-tuple-element.16.zonal_bias_ref), custom_call_target="tpu_custom_call" | custom-call | tf_op jit(solution)/shard_map/convs/pallas_call | solution.py:376
  18.9 0.0 copy-start
  18.9 11.3 %all_to_all.11 = bf16[32,8,384]{2,1,0:T(8,128)(2,1)S(1)} all-to-all(bf16[32,8,384]{2,1,0:T(8,128)(2,1)S(1)} %convs.1), channel_id=1, replica_groups=mesh['face'=4,'sub'=8] {'face','sub'}, dimensions={0} | all-to-all | bytes 393216 | tf_op jit(solution)/shard_map/all_to_all | solution.py:396
  30.2 0.0 copy-done.2
  30.2 0.0 copy-done.1
  30.2 0.0 copy-done
  30.2 1.4 %mlp.1 = bf16[3,4,32,256]{3,2,1,0:T(8,128)(2,1)} custom-call(bf16[256,384]{1,0:T(8,128)(2,1)S(1)} %bitcast.12, bf16[3,4,32,256]{3,2,1,0:T(8,128)(2,1)S(1)} %bitcast.11, f32[1,256]{1,0:T(1,128)S(1)} %get-tuple-element.17.gain_ref, f32[1,256]{1,0:T(1,128)S(1)} %get-tuple-element.18.scale_ref, bf16[256,768]{1,0:T(8,128)(2,1)S(1)} %copy-done.1, ...), custom_call_target="tpu_custom_call" | custom-call | tf_op jit(solution)/shard_map/mlp/pallas_call | solution.py:398
Async XLA Ops:
  1.2 29.0 %copy-start.2 = (bf16[768,256]{1,0:T(8,128)(2,1)S(1)}, bf16[768,256]{1,0:T(8,128)(2,1)}, u32[]{:S(2)}) copy-start(bf16[768,256]{1,0:T(8,128)(2,1)} %w_out_ref.1) | copy-start | bytes 1179652
  17.4 12.8 %copy-start.1 = (bf16[256,768]{1,0:T(8,128)(2,1)S(1)}, bf16[256,768]{1,0:T(8,128)(2,1)}, u32[]{:S(2)}) copy-start(bf16[256,768]{1,0:T(8,128)(2,1)} %w_in_ref.1) | copy-start | bytes 1179652
  18.9 11.3 %copy-start = (bf16[3,1,4,32,256]{4,3,2,1,0:T(8,128)(2,1)S(1)}, bf16[3,1,4,32,256]{4,3,2,1,0:T(8,128)(2,1)}, u32[]{:S(2)}) copy-start(bf16[3,1,4,32,256]{4,3,2,1,0:T(8,128)(2,1)} %param.9) | copy-start | bytes 589828

commit v6 on v5

--- a/solution.py
+++ b/solution.py
@@ -46,7 +46,7 @@
 
 def conv_kernel(
     quads, subs, side, rows, share, axes, x_ref, dw_ref, dw_bias_ref, zonal_ref, zonal_bias_ref, o_ref,
-    e_ref, m_ref, ahead_ref, behind_ref, head_ref, tail_ref, columns, table, w_ref
+    e_ref, m_ref, ahead_ref, behind_ref, columns, table, w_ref
 ):
     lay_out(share, axes, (dw_ref, dw_bias_ref, zonal_ref, zonal_bias_ref), columns, table, w_ref)
     width = quads * side
@@ -152,16 +152,17 @@
         steps.append(step)
         step *= 2
     has_step = {step: (arc & step) != 0 for step in steps}
-    for j in range(quads):
-        back = (quads - j) % quads
-        for d in range(REACH):
-            head_ref[j, d] = jnp.where(northern, m_ref[j, d], m_ref[back, side - 1 - d])
-
-        def join(d, carry, j=j, back=back):
-            tail_ref[j, d] = jnp.where(northern, m_ref[back, side - 1 - d], m_ref[j, d])
-            return carry
-
-        fold(side, join, 0, unroll)
+    kept = {}
+
+    def merged(j, d, tail):
+        key = (j, d, tail)
+        if unroll and key in kept:
+            return kept[key]
+        forth, back = m_ref[j, d], m_ref[wrap(quads - j, quads), side - 1 - d]
+        line = jnp.where(northern, back, forth) if tail else jnp.where(northern, forth, back)
+        if unroll:
+            kept[key] = line
+        return line
 
     def sheared(inputs):
         seen = {}
@@ -184,17 +185,17 @@
         forth_strip, back_strip = wrap(j - 1, quads), wrap(quads + 1 - j, quads)
         heads, tails = {}, {}
         for d in range(REACH):
-            line = head_ref[j, d]
+            line = merged(j, d, False)
             for a in range(1, min(d + 1, REACH)):
-                line = jnp.where(arc == a, head_ref[wrap(j + d // a, quads), d % a], line)
+                line = jnp.where(arc == a, merged(wrap(j + d // a, quads), d % a, False), line)
             heads[d] = line
         for d in range(1, side):
-            tails[d] = tail_ref[j, d]
+            tails[d] = merged(j, d, True)
         for d in range(side, side + REACH - 1):
             line = None
             for a in range(1, side + REACH - d):
                 place = d - side + a
-                moved = tail_ref[wrap(j + place // a, quads), side - a + place % a]
+                moved = merged(wrap(j + place // a, quads), side - a + place % a, True)
                 line = moved if line is None else jnp.where(arc == a, moved, line)
             tails[d] = line
         head, tail = sheared(heads), sheared(tails)
@@ -220,8 +221,9 @@
     def zonal(q, u):
         total = w_ref[17] + w_ref[10 + half] * m_ref[q, u]
         for k in range(1, half + 1):
-            total = total + w_ref[10 + half + k] * ahead_ref[q, u + DILATION * (k - 1)]
-            total = total + w_ref[10 + half - k] * behind_ref[q, side - 1 - u + DILATION * (k - 1)]
+            pair = w_ref[10 + half + k] * ahead_ref[q, u + DILATION * (k - 1)]
+            pair = pair + w_ref[10 + half - k] * behind_ref[q, side - 1 - u + DILATION * (k - 1)]
+            total = total + pair
         return total
 
     def spread(sub, carry):
@@ -383,8 +385,6 @@
             pltpu.VMEM((quads, side, chans, width), jnp.float32),
             pltpu.VMEM((quads, extra, chans, width), jnp.float32),
             pltpu.VMEM((quads, extra, chans, width), jnp.float32),
-            pltpu.VMEM((quads, REACH, chans, width), jnp.float32),
-            pltpu.VMEM((quads, side, chans, width), jnp.float32),
             pltpu.VMEM((channels + chans, 128), jnp.float32),
             pltpu.VMEM((128, channels), jnp.float32),
             pltpu.VMEM((taps, chans, width), jnp.float32),

time: 31.8 us -> 31.8 us (level)
  no operation moved by 1% of the time
where the time goes in v6:
time: 31.8 us; the launch traced here: 31.5 us
  blocking collectives  27.5 us (86%)
  Pallas kernels  4.01 us (13%)
    all_to_all x1, blocking collectives, shards(): lax.all_to_all(packed.reshape(devices, share, cells), ('face', 'sub'), sp...  16.2 us
    all_to_all x1, blocking collectives, shards(): lax.all_to_all(zonal, ('face', 'sub'), split_axis=0, concat_axis=0, tiled...  11.3 us
    pallas_call x1, Pallas kernels, shards(): pl.pallas_call(functools.partial(conv_kernel, quads, subs, side, rows, sh...  1.47 us
    pallas_call x1, Pallas kernels, shards(): pl.pallas_call(mlp_kernel, out_shape=jax.ShapeDtypeStruct(local.shape, jn...  1.4 us
    pallas_call x1, Pallas kernels, shards(): pl.pallas_call(pack_kernel, out_shape=(jax.ShapeDtypeStruct((channels, ce...  1.15 us

profile of v6, /device:TPU:1, one launch (start us, length us, event | category | flops | bytes accessed | tf_op | source)
XLA Modules:
  0.0 31.5 jit_solution(11036365741021630088)
XLA Ops:
  0.0 1.1 %pack.1 = (bf16[256,384]{1,0:T(8,128)(2,1)S(1)}, f32[9,256]{1,0:T(8,128)S(1)}, f32[1,256]{1,0:T(1,128)S(1)}, f32[7,256]{1,0:T(8,128)S(1)}, f32[1,256]{1,0:T(1,12...) custom-call(bf16[3,4,32,256]{3,2,1,0:T(8,128)(2,1)} %bitcast.10, f32[9,256]{1,0:T(8,128)} %refs_0_.1, ...), custom_call_target="tpu_custom_call" | custom-call | tf_op jit(solution)/shard_map/pack/pallas_call | solution.py:356
  1.2 0.0 copy-start.2
  1.2 16.2 %all_to_all.10.x_ref = bf16[32,8,384]{2,1,0:T(8,128)(2,1)S(1)} all-to-all(bf16[32,8,384]{2,1,0:T(8,128)(2,1)S(1)} %bitcast.13), channel_id=1, replica_groups=mesh['face'=4,'sub'=8] {'face','sub'}, dimensions={0} | all-to-all | bytes 393216 | tf_op jit(solution)/shard_map/all_to_all | solution.py:372
  17.4 0.0 copy-start.1
  17.4 1.5 %convs.1 = bf16[32,8,384]{2,1,0:T(8,128)(2,1)S(1)} custom-call(bf16[32,8,384]{2,1,0:T(8,128)(2,1)S(1)} %all_to_all.10.x_ref, f32[9,256]{1,0:T(8,128)S(1)} %get-tuple-element.13.dw_ref, f32[1,256]{1,0:T(1,128)S(1)} %get-tuple-element.14.dw_bias_ref, f32[7,256]{1,0:T(8,128)S(1)} %get-tuple-element.15.zonal_ref, f32[1,256]{1,0:T(1,128)S(1)} %get-tuple-element.16.zonal_bias_ref), custom_call_target="tpu_custom_call" | custom-call | tf_op jit(solution)/shard_map/convs/pallas_call | solution.py:378
  18.8 0.0 copy-start
  18.9 11.3 %all_to_all.11 = bf16[32,8,384]{2,1,0:T(8,128)(2,1)S(1)} all-to-all(bf16[32,8,384]{2,1,0:T(8,128)(2,1)S(1)} %convs.1), channel_id=1, replica_groups=mesh['face'=4,'sub'=8] {'face','sub'}, dimensions={0} | all-to-all | bytes 393216 | tf_op jit(solution)/shard_map/all_to_all | solution.py:396
  30.1 0.0 copy-done.2
  30.1 0.0 copy-done.1
  30.1 0.0 copy-done
  30.1 1.4 %mlp.1 = bf16[3,4,32,256]{3,2,1,0:T(8,128)(2,1)} custom-call(bf16[256,384]{1,0:T(8,128)(2,1)S(1)} %bitcast.12, bf16[3,4,32,256]{3,2,1,0:T(8,128)(2,1)S(1)} %bitcast.11, f32[1,256]{1,0:T(1,128)S(1)} %get-tuple-element.17.gain_ref, f32[1,256]{1,0:T(1,128)S(1)} %get-tuple-element.18.scale_ref, bf16[256,768]{1,0:T(8,128)(2,1)S(1)} %copy-done.1, ...), custom_call_target="tpu_custom_call" | custom-call | tf_op jit(solution)/shard_map/mlp/pallas_call | solution.py:398
Async XLA Ops:
  1.2 29.0 %copy-start.2 = (bf16[768,256]{1,0:T(8,128)(2,1)S(1)}, bf16[768,256]{1,0:T(8,128)(2,1)}, u32[]{:S(2)}) copy-start(bf16[768,256]{1,0:T(8,128)(2,1)} %w_out_ref.1) | copy-start | bytes 1179652
  17.4 12.8 %copy-start.1 = (bf16[256,768]{1,0:T(8,128)(2,1)S(1)}, bf16[256,768]{1,0:T(8,128)(2,1)}, u32[]{:S(2)}) copy-start(bf16[256,768]{1,0:T(8,128)(2,1)} %w_in_ref.1) | copy-start | bytes 1179652
  18.8 11.3 %copy-start = (bf16[3,1,4,32,256]{4,3,2,1,0:T(8,128)(2,1)S(1)}, bf16[3,1,4,32,256]{4,3,2,1,0:T(8,128)(2,1)}, u32[]{:S(2)}) copy-start(bf16[3,1,4,32,256]{4,3,2,1,0:T(8,128)(2,1)} %param.9) | copy-start | bytes 589828

commit v7 on v6

--- a/solution.py
+++ b/solution.py
@@ -48,7 +48,6 @@
     quads, subs, side, rows, share, axes, x_ref, dw_ref, dw_bias_ref, zonal_ref, zonal_bias_ref, o_ref,
     e_ref, m_ref, ahead_ref, behind_ref, columns, table, w_ref
 ):
-    lay_out(share, axes, (dw_ref, dw_bias_ref, zonal_ref, zonal_bias_ref), columns, table, w_ref)
     width = quads * side
     chans = x_ref.shape[1]
     unroll = width <= 128
@@ -111,6 +110,8 @@
             e_ref[after, 1],
             shift_lanes(diagonals[2 * after], width - 1),
         )
+
+    lay_out(share, axes, (dw_ref, dw_bias_ref, zonal_ref, zonal_bias_ref), columns, table, w_ref)
 
     def depthwise(q, u, first=False, last=False):
         below, here, above = e_ref[q, u], e_ref[q, u + 1], e_ref[q, u + 2]

time: 31.8 us -> 31.8 us (level)
  no operation moved by 1% of the time
where the time goes in v7:
time: 31.8 us; the launch traced here: 31.5 us
  blocking collectives  27.5 us (86%)
  Pallas kernels  4 us (13%)
    all_to_all x1, blocking collectives, shards(): lax.all_to_all(packed.reshape(devices, share, cells), ('face', 'sub'), sp...  16.2 us
    all_to_all x1, blocking collectives, shards(): lax.all_to_all(zonal, ('face', 'sub'), split_axis=0, concat_axis=0, tiled...  11.3 us
    pallas_call x1, Pallas kernels, shards(): pl.pallas_call(functools.partial(conv_kernel, quads, subs, side, rows, sh...  1.46 us
    pallas_call x1, Pallas kernels, shards(): pl.pallas_call(mlp_kernel, out_shape=jax.ShapeDtypeStruct(local.shape, jn...  1.4 us
    pallas_call x1, Pallas kernels, shards(): pl.pallas_call(pack_kernel, out_shape=(jax.ShapeDtypeStruct((channels, ce...  1.15 us

profile of v7, /device:TPU:1, one launch (start us, length us, event | category | flops | bytes accessed | tf_op | source)
XLA Modules:
  0.0 31.5 jit_solution(5159629624611508978)
XLA Ops:
  0.0 1.1 %pack.1 = (bf16[256,384]{1,0:T(8,128)(2,1)S(1)}, f32[9,256]{1,0:T(8,128)S(1)}, f32[1,256]{1,0:T(1,128)S(1)}, f32[7,256]{1,0:T(8,128)S(1)}, f32[1,256]{1,0:T(1,12...) custom-call(bf16[3,4,32,256]{3,2,1,0:T(8,128)(2,1)} %bitcast.10, f32[9,256]{1,0:T(8,128)} %refs_0_.1, ...), custom_call_target="tpu_custom_call" | custom-call | tf_op jit(solution)/shard_map/pack/pallas_call | solution.py:357
  1.2 0.0 copy-start.2
  1.2 16.2 %all_to_all.10.x_ref = bf16[32,8,384]{2,1,0:T(8,128)(2,1)S(1)} all-to-all(bf16[32,8,384]{2,1,0:T(8,128)(2,1)S(1)} %bitcast.13), channel_id=1, replica_groups=mesh['face'=4,'sub'=8] {'face','sub'}, dimensions={0} | all-to-all | bytes 393216 | tf_op jit(solution)/shard_map/all_to_all | solution.py:373
  17.4 0.0 copy-start.1
  17.4 1.5 %convs.1 = bf16[32,8,384]{2,1,0:T(8,128)(2,1)S(1)} custom-call(bf16[32,8,384]{2,1,0:T(8,128)(2,1)S(1)} %all_to_all.10.x_ref, f32[9,256]{1,0:T(8,128)S(1)} %get-tuple-element.13.dw_ref, f32[1,256]{1,0:T(1,128)S(1)} %get-tuple-element.14.dw_bias_ref, f32[7,256]{1,0:T(8,128)S(1)} %get-tuple-element.15.zonal_ref, f32[1,256]{1,0:T(1,128)S(1)} %get-tuple-element.16.zonal_bias_ref), custom_call_target="tpu_custom_call" | custom-call | tf_op jit(solution)/shard_map/convs/pallas_call | solution.py:379
  18.8 0.0 copy-start
  18.8 11.3 %all_to_all.11 = bf16[32,8,384]{2,1,0:T(8,128)(2,1)S(1)} all-to-all(bf16[32,8,384]{2,1,0:T(8,128)(2,1)S(1)} %convs.1), channel_id=1, replica_groups=mesh['face'=4,'sub'=8] {'face','sub'}, dimensions={0} | all-to-all | bytes 393216 | tf_op jit(solution)/shard_map/all_to_all | solution.py:397
  30.1 0.0 copy-done.2
  30.1 0.0 copy-done.1
  30.1 0.0 copy-done
  30.1 1.4 %mlp.1 = bf16[3,4,32,256]{3,2,1,0:T(8,128)(2,1)} custom-call(bf16[256,384]{1,0:T(8,128)(2,1)S(1)} %bitcast.12, bf16[3,4,32,256]{3,2,1,0:T(8,128)(2,1)S(1)} %bitcast.11, f32[1,256]{1,0:T(1,128)S(1)} %get-tuple-element.17.gain_ref, f32[1,256]{1,0:T(1,128)S(1)} %get-tuple-element.18.scale_ref, bf16[256,768]{1,0:T(8,128)(2,1)S(1)} %copy-done.1, ...), custom_call_target="tpu_custom_call" | custom-call | tf_op jit(solution)/shard_map/mlp/pallas_call | solution.py:399
Async XLA Ops:
  1.2 29.0 %copy-start.2 = (bf16[768,256]{1,0:T(8,128)(2,1)S(1)}, bf16[768,256]{1,0:T(8,128)(2,1)}, u32[]{:S(2)}) copy-start(bf16[768,256]{1,0:T(8,128)(2,1)} %w_out_ref.1) | copy-start | bytes 1179652
  17.4 12.8 %copy-start.1 = (bf16[256,768]{1,0:T(8,128)(2,1)S(1)}, bf16[256,768]{1,0:T(8,128)(2,1)}, u32[]{:S(2)}) copy-start(bf16[256,768]{1,0:T(8,128)(2,1)} %w_in_ref.1) | copy-start | bytes 1179652
  18.8 11.3 %copy-start = (bf16[3,1,4,32,256]{4,3,2,1,0:T(8,128)(2,1)S(1)}, bf16[3,1,4,32,256]{4,3,2,1,0:T(8,128)(2,1)}, u32[]{:S(2)}) copy-start(bf16[3,1,4,32,256]{4,3,2,1,0:T(8,128)(2,1)} %param.9) | copy-start | bytes 589828

commit v8 on v7

--- a/solution.py
+++ b/solution.py
@@ -298,8 +298,10 @@
 
 
 def mlp_kernel(z_ref, x_ref, gain_ref, scale_ref, w_in_ref, w_out_ref, o_hbm, o_vmem, sems):
-    parts, slots, side, _ = o_vmem.shape
+    _, faces, side, _ = o_vmem.shape
+    slots = faces + 1
     width = slots * side
+    parts = z_ref.shape[1] // width
     gain, scale = gain_ref[...], scale_ref[...]
     stores = []
     for i in range(parts):
@@ -315,17 +317,13 @@
         for k in range(slots):
             face, local = piece_at(i, k)
             source = x_ref[face, local].astype(jnp.float32)
-            place = face if k < slots - 1 else k
-            o_vmem[i, place] = (source + scale * branch[k * side : (k + 1) * side]).astype(jnp.bfloat16)
-        line = piece_at(i, 0)[1]
-        face, local = piece_at(i, slots - 1)
-        for at, (source, target) in enumerate(
-            (
-                (o_vmem.at[i, pl.ds(0, slots - 1)], o_hbm.at[:, line]),
-                (o_vmem.at[i, slots - 1], o_hbm.at[face, local]),
-            )
-        ):
-            store = pltpu.make_async_copy(source, target, sems.at[2 * i + at])
+            part = source + scale * branch[k * side : (k + 1) * side]
+            o_vmem[local, face] = part.astype(jnp.bfloat16)
+        lines = [piece_at(i, 0)[1]]
+        if i % 3 == 2:
+            lines.append(piece_at(i, slots - 1)[1])
+        for line in lines:
+            store = pltpu.make_async_copy(o_vmem.at[line], o_hbm.at[:, line], sems.at[line])
             store.start()
             stores.append(store)
     for store in stores:
@@ -402,8 +400,8 @@
         in_specs=[vmem] * 6,
         out_specs=hbm,
         scratch_shapes=[
-            pltpu.VMEM((cells // width, quads, side, channels), jnp.bfloat16),
-            pltpu.SemaphoreType.DMA((2 * cells // width,)),
+            pltpu.VMEM((rows, faces, side, channels), jnp.bfloat16),
+            pltpu.SemaphoreType.DMA((rows,)),
         ],
         compiler_params=small,
         name="mlp",

time: 31.8 us -> 31.8 us (level)
  no operation moved by 1% of the time
where the time goes in v8:
time: 31.8 us; the launch traced here: 31.5 us
  blocking collectives  27.5 us (86%)
  Pallas kernels  4 us (13%)
    all_to_all x1, blocking collectives, shards(): lax.all_to_all(packed.reshape(devices, share, cells), ('face', 'sub'), sp...  16.2 us
    all_to_all x1, blocking collectives, shards(): lax.all_to_all(zonal, ('face', 'sub'), split_axis=0, concat_axis=0, tiled...  11.3 us
    pallas_call x1, Pallas kernels, shards(): pl.pallas_call(functools.partial(conv_kernel, quads, subs, side, rows, sh...  1.46 us
    pallas_call x1, Pallas kernels, shards(): pl.pallas_call(mlp_kernel, out_shape=jax.ShapeDtypeStruct(local.shape, jn...  1.39 us
    pallas_call x1, Pallas kernels, shards(): pl.pallas_call(pack_kernel, out_shape=(jax.ShapeDtypeStruct((channels, ce...  1.15 us

profile of v8, /device:TPU:1, one launch (start us, length us, event | category | flops | bytes accessed | tf_op | source)
XLA Modules:
  0.0 31.5 jit_solution(6705708661506260180)
XLA Ops:
  0.0 1.1 %pack.1 = (bf16[256,384]{1,0:T(8,128)(2,1)S(1)}, f32[9,256]{1,0:T(8,128)S(1)}, f32[1,256]{1,0:T(1,128)S(1)}, f32[7,256]{1,0:T(8,128)S(1)}, f32[1,256]{1,0:T(1,12...) custom-call(bf16[3,4,32,256]{3,2,1,0:T(8,128)(2,1)} %bitcast.10, f32[9,256]{1,0:T(8,128)} %refs_0_.1, ...), custom_call_target="tpu_custom_call" | custom-call | tf_op jit(solution)/shard_map/pack/pallas_call | solution.py:355
  1.2 0.0 copy-start.2
  1.2 16.2 %all_to_all.10.x_ref = bf16[32,8,384]{2,1,0:T(8,128)(2,1)S(1)} all-to-all(bf16[32,8,384]{2,1,0:T(8,128)(2,1)S(1)} %bitcast.13), channel_id=1, replica_groups=mesh['face'=4,'sub'=8] {'face','sub'}, dimensions={0} | all-to-all | bytes 393216 | tf_op jit(solution)/shard_map/all_to_all | solution.py:371
  17.4 0.0 copy-start.1
  17.4 1.5 %convs.1 = bf16[32,8,384]{2,1,0:T(8,128)(2,1)S(1)} custom-call(bf16[32,8,384]{2,1,0:T(8,128)(2,1)S(1)} %all_to_all.10.x_ref, f32[9,256]{1,0:T(8,128)S(1)} %get-tuple-element.13.dw_ref, f32[1,256]{1,0:T(1,128)S(1)} %get-tuple-element.14.dw_bias_ref, f32[7,256]{1,0:T(8,128)S(1)} %get-tuple-element.15.zonal_ref, f32[1,256]{1,0:T(1,128)S(1)} %get-tuple-element.16.zonal_bias_ref), custom_call_target="tpu_custom_call" | custom-call | tf_op jit(solution)/shard_map/convs/pallas_call | solution.py:377
  18.8 0.0 copy-start
  18.8 11.3 %all_to_all.11 = bf16[32,8,384]{2,1,0:T(8,128)(2,1)S(1)} all-to-all(bf16[32,8,384]{2,1,0:T(8,128)(2,1)S(1)} %convs.1), channel_id=1, replica_groups=mesh['face'=4,'sub'=8] {'face','sub'}, dimensions={0} | all-to-all | bytes 393216 | tf_op jit(solution)/shard_map/all_to_all | solution.py:395
  30.1 0.0 copy-done.2
  30.1 0.0 copy-done.1
  30.1 0.0 copy-done
  30.1 1.4 %mlp.1 = bf16[3,4,32,256]{3,2,1,0:T(8,128)(2,1)} custom-call(bf16[256,384]{1,0:T(8,128)(2,1)S(1)} %bitcast.12, bf16[3,4,32,256]{3,2,1,0:T(8,128)(2,1)S(1)} %bitcast.11, f32[1,256]{1,0:T(1,128)S(1)} %get-tuple-element.17.gain_ref, f32[1,256]{1,0:T(1,128)S(1)} %get-tuple-element.18.scale_ref, bf16[256,768]{1,0:T(8,128)(2,1)S(1)} %copy-done.1, ...), custom_call_target="tpu_custom_call" | custom-call | tf_op jit(solution)/shard_map/mlp/pallas_call | solution.py:397
Async XLA Ops:
  1.2 29.0 %copy-start.2 = (bf16[768,256]{1,0:T(8,128)(2,1)S(1)}, bf16[768,256]{1,0:T(8,128)(2,1)}, u32[]{:S(2)}) copy-start(bf16[768,256]{1,0:T(8,128)(2,1)} %w_out_ref.1) | copy-start | bytes 1179652
  17.4 12.8 %copy-start.1 = (bf16[256,768]{1,0:T(8,128)(2,1)S(1)}, bf16[256,768]{1,0:T(8,128)(2,1)}, u32[]{:S(2)}) copy-start(bf16[256,768]{1,0:T(8,128)(2,1)} %w_in_ref.1) | copy-start | bytes 1179652
  18.8 11.3 %copy-start = (bf16[3,1,4,32,256]{4,3,2,1,0:T(8,128)(2,1)S(1)}, bf16[3,1,4,32,256]{4,3,2,1,0:T(8,128)(2,1)}, u32[]{:S(2)}) copy-start(bf16[3,1,4,32,256]{4,3,2,1,0:T(8,128)(2,1)} %param.9) | copy-start | bytes 589828

commit v9 on v7

--- a/solution.py
+++ b/solution.py
@@ -289,12 +289,14 @@
     ]
     for copy in small + loads:
         copy.start()
-    for copy in small + loads:
+    for copy in loads:
         copy.wait()
     width = 4 * side
     for block in range(3 * rows // 4):
         pieces = [x_vmem[local, face] for face, local in (piece_at(block, k) for k in range(4))]
         o_ref[:, block * width : (block + 1) * width] = jnp.concatenate(pieces, 0).T
+    for copy in small:
+        copy.wait()
 
 
 def mlp_kernel(z_ref, x_ref, gain_ref, scale_ref, w_in_ref, w_out_ref, o_hbm, o_vmem, sems):

time: 31.8 us -> 31.8 us (level)
  no operation moved by 1% of the time
where the time goes in v9:
time: 31.8 us; the launch traced here: 31.5 us
  blocking collectives  27.5 us (86%)
  Pallas kernels  4.01 us (13%)
    all_to_all x1, blocking collectives, shards(): lax.all_to_all(packed.reshape(devices, share, cells), ('face', 'sub'), sp...  16.2 us
    all_to_all x1, blocking collectives, shards(): lax.all_to_all(zonal, ('face', 'sub'), split_axis=0, concat_axis=0, tiled...  11.3 us
    pallas_call x1, Pallas kernels, shards(): pl.pallas_call(functools.partial(conv_kernel, quads, subs, side, rows, sh...  1.46 us
    pallas_call x1, Pallas kernels, shards(): pl.pallas_call(mlp_kernel, out_shape=jax.ShapeDtypeStruct(local.shape, jn...  1.4 us
    pallas_call x1, Pallas kernels, shards(): pl.pallas_call(pack_kernel, out_shape=(jax.ShapeDtypeStruct((channels, ce...  1.16 us

profile of v9, /device:TPU:1, one launch (start us, length us, event | category | flops | bytes accessed | tf_op | source)
XLA Modules:
  0.0 31.5 jit_solution(5895735819865815441)
XLA Ops:
  0.0 1.2 %pack.1 = (bf16[256,384]{1,0:T(8,128)(2,1)S(1)}, f32[9,256]{1,0:T(8,128)S(1)}, f32[1,256]{1,0:T(1,128)S(1)}, f32[7,256]{1,0:T(8,128)S(1)}, f32[1,256]{1,0:T(1,12...) custom-call(bf16[3,4,32,256]{3,2,1,0:T(8,128)(2,1)} %bitcast.10, f32[9,256]{1,0:T(8,128)} %refs_0_.1, ...), custom_call_target="tpu_custom_call" | custom-call | tf_op jit(solution)/shard_map/pack/pallas_call | solution.py:359
  1.2 0.0 copy-start.2
  1.2 16.2 %all_to_all.10.x_ref = bf16[32,8,384]{2,1,0:T(8,128)(2,1)S(1)} all-to-all(bf16[32,8,384]{2,1,0:T(8,128)(2,1)S(1)} %bitcast.13), channel_id=1, replica_groups=mesh['face'=4,'sub'=8] {'face','sub'}, dimensions={0} | all-to-all | bytes 393216 | tf_op jit(solution)/shard_map/all_to_all | solution.py:375
  17.4 0.0 copy-start.1
  17.4 1.5 %convs.1 = bf16[32,8,384]{2,1,0:T(8,128)(2,1)S(1)} custom-call(bf16[32,8,384]{2,1,0:T(8,128)(2,1)S(1)} %all_to_all.10.x_ref, f32[9,256]{1,0:T(8,128)S(1)} %get-tuple-element.13.dw_ref, f32[1,256]{1,0:T(1,128)S(1)} %get-tuple-element.14.dw_bias_ref, f32[7,256]{1,0:T(8,128)S(1)} %get-tuple-element.15.zonal_ref, f32[1,256]{1,0:T(1,128)S(1)} %get-tuple-element.16.zonal_bias_ref), custom_call_target="tpu_custom_call" | custom-call | tf_op jit(solution)/shard_map/convs/pallas_call | solution.py:381
  18.8 0.0 copy-start
  18.9 11.3 %all_to_all.11 = bf16[32,8,384]{2,1,0:T(8,128)(2,1)S(1)} all-to-all(bf16[32,8,384]{2,1,0:T(8,128)(2,1)S(1)} %convs.1), channel_id=1, replica_groups=mesh['face'=4,'sub'=8] {'face','sub'}, dimensions={0} | all-to-all | bytes 393216 | tf_op jit(solution)/shard_map/all_to_all | solution.py:399
  30.1 0.0 copy-done.2
  30.1 0.0 copy-done.1
  30.1 0.0 copy-done
  30.1 1.4 %mlp.1 = bf16[3,4,32,256]{3,2,1,0:T(8,128)(2,1)} custom-call(bf16[256,384]{1,0:T(8,128)(2,1)S(1)} %bitcast.12, bf16[3,4,32,256]{3,2,1,0:T(8,128)(2,1)S(1)} %bitcast.11, f32[1,256]{1,0:T(1,128)S(1)} %get-tuple-element.17.gain_ref, f32[1,256]{1,0:T(1,128)S(1)} %get-tuple-element.18.scale_ref, bf16[256,768]{1,0:T(8,128)(2,1)S(1)} %copy-done.1, ...), custom_call_target="tpu_custom_call" | custom-call | tf_op jit(solution)/shard_map/mlp/pallas_call | solution.py:401
Async XLA Ops:
  1.2 29.0 %copy-start.2 = (bf16[768,256]{1,0:T(8,128)(2,1)S(1)}, bf16[768,256]{1,0:T(8,128)(2,1)}, u32[]{:S(2)}) copy-start(bf16[768,256]{1,0:T(8,128)(2,1)} %w_out_ref.1) | copy-start | bytes 1179652
  17.4 12.8 %copy-start.1 = (bf16[256,768]{1,0:T(8,128)(2,1)S(1)}, bf16[256,768]{1,0:T(8,128)(2,1)}, u32[]{:S(2)}) copy-start(bf16[256,768]{1,0:T(8,128)(2,1)} %w_in_ref.1) | copy-start | bytes 1179652
  18.8 11.3 %copy-start = (bf16[3,1,4,32,256]{4,3,2,1,0:T(8,128)(2,1)S(1)}, bf16[3,1,4,32,256]{4,3,2,1,0:T(8,128)(2,1)}, u32[]{:S(2)}) copy-start(bf16[3,1,4,32,256]{4,3,2,1,0:T(8,128)(2,1)} %param.9) | copy-start | bytes 589828

commit v10 on v7

--- a/solution.py
+++ b/solution.py
@@ -310,7 +310,8 @@
         values = values * lax.rsqrt(spread + EPSILON)
         normed = (values.T * gain).astype(jnp.bfloat16)
         inner = jnp.dot(normed, w_in_ref[...], preferred_element_type=jnp.float32)
-        hidden = (0.5 * inner * (1.0 + lax.erf(inner * 0.5**0.5))).astype(jnp.bfloat16)
+        half = 0.5 * inner
+        hidden = (half + half * lax.erf(inner * 0.5**0.5)).astype(jnp.bfloat16)
         branch = jnp.dot(hidden, w_out_ref[...], preferred_element_type=jnp.float32)
         for k in range(slots):
             face, local = piece_at(i, k)

time: 31.8 us -> 31.8 us (level)
  no operation moved by 1% of the time
where the time goes in v10:
time: 31.8 us; the launch traced here: 31.5 us
  blocking collectives  27.5 us (86%)
  Pallas kernels  4 us (13%)
    all_to_all x1, blocking collectives, shards(): lax.all_to_all(packed.reshape(devices, share, cells), ('face', 'sub'), sp...  16.2 us
    all_to_all x1, blocking collectives, shards(): lax.all_to_all(zonal, ('face', 'sub'), split_axis=0, concat_axis=0, tiled...  11.3 us
    pallas_call x1, Pallas kernels, shards(): pl.pallas_call(functools.partial(conv_kernel, quads, subs, side, rows, sh...  1.46 us
    pallas_call x1, Pallas kernels, shards(): pl.pallas_call(mlp_kernel, out_shape=jax.ShapeDtypeStruct(local.shape, jn...  1.4 us
    pallas_call x1, Pallas kernels, shards(): pl.pallas_call(pack_kernel, out_shape=(jax.ShapeDtypeStruct((channels, ce...  1.15 us

profile of v10, /device:TPU:1, one launch (start us, length us, event | category | flops | bytes accessed | tf_op | source)
XLA Modules:
  0.0 31.5 jit_solution(11882787841749223383)
XLA Ops:
  0.0 1.1 %pack.1 = (bf16[256,384]{1,0:T(8,128)(2,1)S(1)}, f32[9,256]{1,0:T(8,128)S(1)}, f32[1,256]{1,0:T(1,128)S(1)}, f32[7,256]{1,0:T(8,128)S(1)}, f32[1,256]{1,0:T(1,12...) custom-call(bf16[3,4,32,256]{3,2,1,0:T(8,128)(2,1)} %bitcast.10, f32[9,256]{1,0:T(8,128)} %refs_0_.1, ...), custom_call_target="tpu_custom_call" | custom-call | tf_op jit(solution)/shard_map/pack/pallas_call | solution.py:358
  1.2 0.0 copy-start.2
  1.2 16.2 %all_to_all.10.x_ref = bf16[32,8,384]{2,1,0:T(8,128)(2,1)S(1)} all-to-all(bf16[32,8,384]{2,1,0:T(8,128)(2,1)S(1)} %bitcast.13), channel_id=1, replica_groups=mesh['face'=4,'sub'=8] {'face','sub'}, dimensions={0} | all-to-all | bytes 393216 | tf_op jit(solution)/shard_map/all_to_all | solution.py:374
  17.4 0.0 copy-start.1
  17.4 1.5 %convs.1 = bf16[32,8,384]{2,1,0:T(8,128)(2,1)S(1)} custom-call(bf16[32,8,384]{2,1,0:T(8,128)(2,1)S(1)} %all_to_all.10.x_ref, f32[9,256]{1,0:T(8,128)S(1)} %get-tuple-element.13.dw_ref, f32[1,256]{1,0:T(1,128)S(1)} %get-tuple-element.14.dw_bias_ref, f32[7,256]{1,0:T(8,128)S(1)} %get-tuple-element.15.zonal_ref, f32[1,256]{1,0:T(1,128)S(1)} %get-tuple-element.16.zonal_bias_ref), custom_call_target="tpu_custom_call" | custom-call | tf_op jit(solution)/shard_map/convs/pallas_call | solution.py:380
  18.8 0.0 copy-start
  18.8 11.3 %all_to_all.11 = bf16[32,8,384]{2,1,0:T(8,128)(2,1)S(1)} all-to-all(bf16[32,8,384]{2,1,0:T(8,128)(2,1)S(1)} %convs.1), channel_id=1, replica_groups=mesh['face'=4,'sub'=8] {'face','sub'}, dimensions={0} | all-to-all | bytes 393216 | tf_op jit(solution)/shard_map/all_to_all | solution.py:398
  30.1 0.0 copy-done.2
  30.1 0.0 copy-done.1
  30.1 0.0 copy-done
  30.1 1.4 %mlp.1 = bf16[3,4,32,256]{3,2,1,0:T(8,128)(2,1)} custom-call(bf16[256,384]{1,0:T(8,128)(2,1)S(1)} %bitcast.12, bf16[3,4,32,256]{3,2,1,0:T(8,128)(2,1)S(1)} %bitcast.11, f32[1,256]{1,0:T(1,128)S(1)} %get-tuple-element.17.gain_ref, f32[1,256]{1,0:T(1,128)S(1)} %get-tuple-element.18.scale_ref, bf16[256,768]{1,0:T(8,128)(2,1)S(1)} %copy-done.1, ...), custom_call_target="tpu_custom_call" | custom-call | tf_op jit(solution)/shard_map/mlp/pallas_call | solution.py:400
Async XLA Ops:
  1.2 29.0 %copy-start.2 = (bf16[768,256]{1,0:T(8,128)(2,1)S(1)}, bf16[768,256]{1,0:T(8,128)(2,1)}, u32[]{:S(2)}) copy-start(bf16[768,256]{1,0:T(8,128)(2,1)} %w_out_ref.1) | copy-start | bytes 1179652
  17.4 12.8 %copy-start.1 = (bf16[256,768]{1,0:T(8,128)(2,1)S(1)}, bf16[256,768]{1,0:T(8,128)(2,1)}, u32[]{:S(2)}) copy-start(bf16[256,768]{1,0:T(8,128)(2,1)} %w_in_ref.1) | copy-start | bytes 1179652
  18.8 11.3 %copy-start = (bf16[3,1,4,32,256]{4,3,2,1,0:T(8,128)(2,1)S(1)}, bf16[3,1,4,32,256]{4,3,2,1,0:T(8,128)(2,1)}, u32[]{:S(2)}) copy-start(bf16[3,1,4,32,256]{4,3,2,1,0:T(8,128)(2,1)} %param.9) | copy-start | bytes 589828
